TPU v7x, 1024 devices: a whole 4x8x16 slice. The times are simulated.
1024 devices in a mesh: mem: 4 (over z_hi), lat: 256 (over z_lo, y, x, core).
Axes of the slice: x: 4, y: 8, z: 16 (z_hi: 4, z_lo: 4; z = z_hi * 4 + z_lo), core: 2. Of those that a mesh axis runs over, the one named last changes fastest.
Arguments:
- states: bfloat16 [64, 5, 1024, 4, 128], P('mem', None, 'lat'), may hold values from -6 to 6
- src_ids: int32 [4, 8], P('mem'), may hold values from 0 to 15, as said below
- coarse_w: float32 [512, 16, 32, 64], P('lat', None, None, 'mem'), may hold values from -1 to 1
- lon_cell: int32 [128], replicated, may hold values from 0 to 14, as said below
- lon_frac: float32 [128], replicated, may hold values from 0 to 1
- viscosity: float32 [4, 128], replicated, may hold values from 0.02 to 0.25
Outputs:
- forecast: float32 [64, 5, 1024, 4, 128], P('mem', None, 'lat')
Inputs may be any that keep to these rules, and one draw needn't show every extreme that they name: `src_ids`: each group's row names 8 different members of that group by their index within it. `lon_cell`: never falls along longitude.
All inputs are finite; a program needn't handle non-finite values.
Results may differ from a plain program's by a relative error of at most 0.0003.
Values may be sent and summed in bfloat16 or wider, within the bound.
No kernel may reach another device: no remote copies, remote signals or barrier semaphores. Data moves between devices by JAX's collectives and lax.ppermute only.
A program may use at most 128 MiB of HBM per device.

v0:
```python
import jax
import jax.numpy as jnp
from jax import lax
from jax.sharding import PartitionSpec as P

time_step = 0.25


def spread(block, axis, source):
    block = jnp.where(lax.axis_index(axis) == source, block, jnp.zeros_like(block))
    return lax.psum(block, axis)


def padded_2(array, sides, width):
    for axis, dim in sides:
        size, length = (lax.axis_size(axis), array.shape[dim])
        up = [(i, (i + 1) % size) for i in range(size - 1)]
        down = [(j, i) for i, j in up]
        last = lax.slice_in_dim(array, length - width, length, axis=dim)
        initial = lax.slice_in_dim(array, 0, width, axis=dim)
        before = lax.ppermute(last, axis, up)
        after = lax.ppermute(initial, axis, down)
        array = jnp.concatenate([before, array, after], axis=dim)
    return array


def advance(padded, viscosity):
    centre = padded[..., 1:-1, :, :]
    north = padded[..., 2:, :, :]
    south = padded[..., :-2, :, :]
    east = jnp.roll(centre, -1, axis=-1)
    west = jnp.roll(centre, 1, axis=-1)
    dx_all = (east - west) * 0.5
    dy_all = (north - south) * 0.5
    lap_all = east + west + north + south - 4.0 * centre
    u_wind = centre[..., 0:1, :, :, :]
    v_wind = centre[..., 1:2, :, :, :]
    tend = -(u_wind * dx_all + v_wind * dy_all) + viscosity * lap_all
    zero_part = jnp.zeros_like(centre[..., 0:2, :, :, :])
    extra = jnp.concatenate(
        [
            -dx_all[..., 2:3, :, :, :],
            -dy_all[..., 2:3, :, :, :],
            -(dx_all[..., 0:1, :, :, :] + dy_all[..., 1:2, :, :, :]),
            zero_part,
        ],
        axis=-4,
    )
    return centre + time_step * (tend + extra)


def interp_weights(coarse_rows, table, rows):
    bands = coarse_rows.shape[0] // 2
    flat_w = coarse_rows.reshape(coarse_rows.shape[0], coarse_rows.shape[1], -1)
    lon_w = jnp.einsum("nc,rcx->rnx", table, flat_w, precision=lax.Precision.HIGHEST)
    lon_w = lon_w.reshape(bands, 2, table.shape[0], coarse_rows.shape[2], coarse_rows.shape[3])
    frac = (jnp.arange(rows, dtype=jnp.float32) + 0.5) / rows
    lower = lon_w[:, 0][:, None]
    higher = lon_w[:, 1][:, None]
    return (1.0 - frac)[None, :, None, None, None] * lower + frac[
        None, :, None, None, None
    ] * higher


def on_device(states, src_ids, coarse_w, lon_cell, lon_frac, viscosity):
    rows = states.shape[2]
    groups = lax.axis_size("mem")
    own_ids = src_ids[0]
    picked = states[own_ids]
    pieces = []
    for owner in range(groups):
        pieces.append(spread(picked, "mem", owner))
    sources = jnp.concatenate(pieces, axis=0)
    points = jnp.arange(coarse_w.shape[1], dtype=jnp.int32)
    lower = lon_cell[:, None] == points[None, :]
    upper = lon_cell[:, None] + 1 == points[None, :]
    table = jnp.where(lower, 1.0 - lon_frac[:, None], 0.0) + jnp.where(
        upper, lon_frac[:, None], 0.0
    )
    weights = interp_weights(coarse_w, table, rows)[0]
    field = jnp.einsum(
        "rnsk,sfrln->kfrln", weights, sources.astype(jnp.float32), precision=lax.Precision.HIGHEST
    )
    for step in range(2):
        padded = padded_2(field, (("lat", 2),), 1)
        field = advance(padded, viscosity)
    return field


def solution(mesh):
    in_specs = (
        P("mem", None, "lat", None, None),
        P("mem", None),
        P("lat", None, None, "mem"),
        P(),
        P(),
        P(),
    )
    out_specs = P("mem", None, "lat", None, None)
    return jax.shard_map(
        on_device, mesh=mesh, in_specs=in_specs, out_specs=out_specs, check_vma=False
    )
```

profile of v0, /device:TPU:64, one launch (start us, length us, event | category | flops | bytes accessed | tf_op | source)
XLA Modules:
  0.0 183.9 jit_solution(1446656099538795501)
XLA Ops:
  6.5 0.0 copy-start
  6.5 0.0 all-reduce.3.cloned.1.call-start
  6.5 0.7 fusion.32
  7.3 0.3 copy-done
  7.5 0.7 gather_fusion
  8.2 0.9 broadcast_select_fusion.3
  9.1 0.0 all-reduce.3.cloned.1.call-update
  9.1 0.7 broadcast_add_fusion
  9.8 0.7 broadcast_subtract_fusion
  10.4 1.2 copy.150
  11.6 0.3 reshape.68
  11.9 1.3 convolution_bitcast_fusion
  13.2 0.2 copy.151
  13.4 0.5 copy.152
  14.0 0.5 copy.153
  14.5 0.1 pad.15.clone
  14.6 103.3 %all-reduce.3.cloned.1.call-done = (bf16[8,5,4,4,128]{4,0,3,2,1:T(8,128)(2,1)}, bf16[8,5,4,4,128]{4,0,3,2,1:T(8,128)(2,1)}, bf16[8,5,4,4,128]{4,0,3,2,1:T(8,128)(2,1)}, bf16[8,5,4,4,128]{4,0,3,2,1:T(8,128)(2,1)}) async-done(((bf16[8,5,4,4,128]{4,0,3,2,1:T(8,128)(2,1)}, bf16[8,5,4,4,128]{4,0,3,2,1:T(8,128)(2,1)}, bf16[8,5,4,4,128]{4,0,3,2,1:T(8,128)(2,1)}, bf16[8,5,4,4,128]{4,0,3,2,1:T(8,128)(2,1)}), ...) | async-done | bytes 655376 | tf_op jit(solution)/shard_map/psum | solution.py:11
  117.9 1.3 pad_maximum_fusion.4
  119.2 6.5 %copy.154 = bf16[32,5,4,4,128]{0,1,3,4,2:T(8,128)(2,1)} copy(bf16[32,5,4,4,128]{4,0,3,2,1:T(8,128)(2,1)S(1)} %pad_maximum_fusion.4) | data formatting | bytes 1310720 | tf_op jit(solution)/shard_map/concatenate | solution.py:73
  125.7 11.0 %fusion = f32[4,128,5,4,16]{4,2,3,1,0:T(8,128)} fusion(bf16[32,5,4,4,128]{0,1,3,4,2:T(8,128)(2,1)} %copy.154, f32[128,32,16]{1,2,0:T(8,128)S(1)} %copy.153, f32[4]{0:T(128)S(1)} %get-tuple-element.37, f32[128,32,16]{1,2,0:T(8,128)S(1)} %copy.152, f32[4]{0:T(128)S(1)} %get-tuple-element.38), kind=kOutput, calls=%fused_computation.1 | convolution fusion | flops 63700992 | bytes 1835040 | tf_op jit(solution)/shard_map/rnsk,sfrln->kfrln/dot_general | solution.py:81
  136.6 5.4 %copy.155 = f32[4,128,5,4,16]{1,4,3,0,2:T(8,128)S(1)} copy(f32[4,128,5,4,16]{4,2,3,1,0:T(8,128)} %fusion) | data formatting | bytes 1310720 | tf_op jit(solution)/shard_map/rnsk,sfrln->kfrln/dot_general | solution.py:81
  142.0 0.2 fusion.37
  142.3 0.0 copy-start.1
  142.3 0.2 fusion.38
  142.5 7.7 %collective-permute-start = (f32[16,5,1,4,128]{4,0,3,2,1:T(8,128)S(1)}, f32[16,5,1,4,128]{4,0,3,2,1:T(8,128)S(1)}, u32[]{:S(2)}, u32[]{:S(2)}) collective-permute-start(f32[16,5,1,4,128]{4,0,3,2,1:T(8,128)S(1)} %get-tuple-element.30), channel_id=1, source_target_pairs={{1,0},{2,1},{3,2},{4,3},{5,4},{6,5},{7,6},{8,7},{9,8},{10,9},{11,1... | collective-permute-start | bytes 491528 | tf_op jit(solution)/shard_map/ppermute | solution.py:22
  150.3 1.9 %collective-permute-start.1 = (f32[16,5,1,4,128]{4,0,3,2,1:T(8,128)S(1)}, f32[16,5,1,4,128]{4,0,3,2,1:T(8,128)S(1)}, u32[]{:S(2)}, u32[]{:S(2)}) collective-permute-start(f32[16,5,1,4,128]{4,0,3,2,1:T(8,128)S(1)} %get-tuple-element.29), channel_id=1, source_target_pairs={{0,1},{1,2},{2,3},{3,4},{4,5},{5,6},{6,7},{7,8},{8,9},{9,10},{10,1... | collective-permute-start | bytes 491528 | tf_op jit(solution)/shard_map/ppermute | solution.py:21
  152.2 0.4 broadcast_multiply_fusion.1
  152.7 0.4 collective-permute-done
  153.1 8.0 %collective-permute-done.1 = f32[16,5,1,4,128]{4,0,3,2,1:T(8,128)S(1)} collective-permute-done((f32[16,5,1,4,128]{4,0,3,2,1:T(8,128)S(1)}, f32[16,5,1,4,128]{4,0,3,2,1:T(8,128)S(1)}, u32[]{:S(2)}, u32[]{:S(2)}) %collective-permute-start.1) | collective-permute-done | bytes 163872 | tf_op jit(solution)/shard_map/ppermute | solution.py:21
  161.1 0.1 fusion.14
  161.3 0.0 copy-done.1
  161.3 0.6 fusion.10
  162.0 0.2 fusion.34
  162.2 0.2 fusion.35
  162.5 1.9 %collective-permute-start.2 = (f32[16,5,1,4,128]{4,0,3,2,1:T(8,128)S(1)}, f32[16,5,1,4,128]{4,0,3,2,1:T(8,128)S(1)}, u32[]{:S(2)}, u32[]{:S(2)}) collective-permute-start(f32[16,5,1,4,128]{4,0,3,2,1:T(8,128)S(1)} %get-tuple-element.19), channel_id=1, source_target_pairs={{1,0},{2,1},{3,2},{4,3},{5,4},{6,5},{7,6},{8,7},{9,8},{10,9},{11,1... | collective-permute-start | bytes 491528 | tf_op jit(solution)/shard_map/ppermute | solution.py:22
  164.4 2.4 %collective-permute-start.3 = (f32[16,5,1,4,128]{4,0,3,2,1:T(8,128)S(1)}, f32[16,5,1,4,128]{4,0,3,2,1:T(8,128)S(1)}, u32[]{:S(2)}, u32[]{:S(2)}) collective-permute-start(f32[16,5,1,4,128]{4,0,3,2,1:T(8,128)S(1)} %get-tuple-element.18), channel_id=1, source_target_pairs={{0,1},{1,2},{2,3},{3,4},{4,5},{5,6},{6,7},{7,8},{8,9},{9,10},{10,1... | collective-permute-start | bytes 491528 | tf_op jit(solution)/shard_map/ppermute | solution.py:21
  166.8 0.4 broadcast_multiply_fusion
  167.3 0.0 collective-permute-done.2
  167.3 8.0 %collective-permute-done.3 = f32[16,5,1,4,128]{4,0,3,2,1:T(8,128)S(1)} collective-permute-done((f32[16,5,1,4,128]{4,0,3,2,1:T(8,128)S(1)}, f32[16,5,1,4,128]{4,0,3,2,1:T(8,128)S(1)}, u32[]{:S(2)}, u32[]{:S(2)}) %collective-permute-start.3) | collective-permute-done | bytes 163872 | tf_op jit(solution)/shard_map/ppermute | solution.py:21
  175.3 0.1 fusion.16
  175.4 0.6 fusion.12
  176.0 1.1 copy.156
  (10 shorter events, 0.2 us)
Async XLA Ops:
  6.5 1.0 copy-start
  6.5 111.4 %all-reduce.3.cloned.1.call-start = ((), (), s32[]{:S(2)}) async-start(), calls=%async_computation | async-start | bytes 1310720 | tf_op jit(solution)/shard_map/psum | solution.py:11
  142.3 19.0 %copy-start.1 = (f32[4,128]{1,0:T(4,128)S(1)}, f32[4,128]{1,0:T(4,128)}, u32[]{:S(2)}) copy-start(f32[4,128]{1,0:T(4,128)} %param.11) | copy-start | bytes 6148
  142.5 10.6 %collective-permute-start = (f32[16,5,1,4,128]{4,0,3,2,1:T(8,128)S(1)}, f32[16,5,1,4,128]{4,0,3,2,1:T(8,128)S(1)}, u32[]{:S(2)}, u32[]{:S(2)}) collective-permute-start(f32[16,5,1,4,128]{4,0,3,2,1:T(8,128)S(1)} %get-tuple-element.30), channel_id=1, source_target_pairs={{1,0},{2,1},{3,2},{4,3},{5,4},{6,5},{7,6},{8,7},{9,8},{10,9},{11,1... | collective-permute-start | bytes 491528 | tf_op jit(solution)/shard_map/ppermute | solution.py:22
  150.3 10.9 %collective-permute-start.1 = (f32[16,5,1,4,128]{4,0,3,2,1:T(8,128)S(1)}, f32[16,5,1,4,128]{4,0,3,2,1:T(8,128)S(1)}, u32[]{:S(2)}, u32[]{:S(2)}) collective-permute-start(f32[16,5,1,4,128]{4,0,3,2,1:T(8,128)S(1)} %get-tuple-element.29), channel_id=1, source_target_pairs={{0,1},{1,2},{2,3},{3,4},{4,5},{5,6},{6,7},{7,8},{8,9},{9,10},{10,1... | collective-permute-start | bytes 491528 | tf_op jit(solution)/shard_map/ppermute | solution.py:21
  162.5 4.8 %collective-permute-start.2 = (f32[16,5,1,4,128]{4,0,3,2,1:T(8,128)S(1)}, f32[16,5,1,4,128]{4,0,3,2,1:T(8,128)S(1)}, u32[]{:S(2)}, u32[]{:S(2)}) collective-permute-start(f32[16,5,1,4,128]{4,0,3,2,1:T(8,128)S(1)} %get-tuple-element.19), channel_id=1, source_target_pairs={{1,0},{2,1},{3,2},{4,3},{5,4},{6,5},{7,6},{8,7},{9,8},{10,9},{11,1... | collective-permute-start | bytes 491528 | tf_op jit(solution)/shard_map/ppermute | solution.py:22
  164.4 10.9 %collective-permute-start.3 = (f32[16,5,1,4,128]{4,0,3,2,1:T(8,128)S(1)}, f32[16,5,1,4,128]{4,0,3,2,1:T(8,128)S(1)}, u32[]{:S(2)}, u32[]{:S(2)}) collective-permute-start(f32[16,5,1,4,128]{4,0,3,2,1:T(8,128)S(1)} %get-tuple-element.18), channel_id=1, source_target_pairs={{0,1},{1,2},{2,3},{3,4},{4,5},{5,6},{6,7},{7,8},{8,9},{9,10},{10,1... | collective-permute-start | bytes 491528 | tf_op jit(solution)/shard_map/ppermute | solution.py:21
Sparse Core Ops, SparseCore 0:
  11.1 106.7 all-reduce.2
where the time goes:
time: 184 us
  waiting for transfers between devices  120 us (65%)
  local copies, waits for them, and re-layouts  17.8 us (10%)
  starting transfers between devices  14 us (8%)
  between operations  13.6 us (7%)
  matrix products  12.3 us (7%)
  other arithmetic  6.53 us (4%)
    psum x1, waiting for transfers between devices, spread(): return lax.psum(block, axis)  103 us
    ppermute x2, waiting for transfers between devices, padded_2(): before = lax.ppermute(last, axis, up)  16 us
    dot_general x1, matrix products, on_device(): jnp.einsum('rnsk,sfrln->kfrln', weights, sources.astype(jnp.float32), pre...  11 us
    ppermute x2, starting transfers between devices, padded_2(): after = lax.ppermute(initial, axis, down)  9.66 us
    concatenate x1, local copies, waits for them, and re-layouts, on_device(): sources = jnp.concatenate(pieces, axis=0)  6.46 us
    dot_general x1, local copies, waits for them, and re-layouts, on_device(): jnp.einsum('rnsk,sfrln->kfrln', weights, sources.astype(jnp.float32), pre...  5.39 us
    ppermute x2, starting transfers between devices, padded_2(): before = lax.ppermute(last, axis, up)  4.33 us
  transfers between devices with their start and end apart: 5, of which 4 were waited for; matrix products, arithmetic and copies ran while one was open for 3% of the time, Pallas kernels for 0%

commit v1 on v0

v1 whole, which is shorter than its diff:
```python
import functools

import jax
import jax.numpy as jnp
from jax import lax
from jax.experimental import pallas as pl
from jax.experimental.pallas import tpu as pltpu
from jax.sharding import PartitionSpec as P

ROWS = 4
LEV = 4
FIELDS = 5
VMEM_LIMIT = 48 * 1024 * 1024
VMEM = pl.BlockSpec(memory_space=pltpu.VMEM)
SMEM = pl.BlockSpec(memory_space=pltpu.SMEM)


def pick_kernel(ids_ref, states_ref, out_ref, sem):
    n = out_ref.shape[0]
    copies = []
    for i in range(n):
        copy = pltpu.make_async_copy(states_ref.at[ids_ref[0, i]], out_ref.at[i], sem.at[i])
        copy.start()
        copies.append(copy)
    for copy in copies:
        copy.wait()


def pick(states, src_ids):
    n = src_ids.shape[1]
    return pl.pallas_call(
        pick_kernel,
        out_shape=jax.ShapeDtypeStruct((n,) + states.shape[1:], states.dtype),
        in_specs=[SMEM, pl.BlockSpec(memory_space=pl.ANY)],
        out_specs=pl.BlockSpec(memory_space=pl.ANY),
        scratch_shapes=[pltpu.SemaphoreType.DMA((n,))],
        name="pick",
    )(src_ids, states)


def make_weights(coarse_ref, cell_ref, frac_ref, weights_ref, members):
    nlon = cell_ref.shape[1]
    points = coarse_ref.shape[0] // (2 * members)
    point = lax.broadcasted_iota(jnp.int32, (points, nlon), 0)
    cell = jnp.broadcast_to(cell_ref[...], (points, nlon))
    frac = jnp.broadcast_to(frac_ref[...], (points, nlon))
    table = jnp.where(cell == point, 1.0 - frac, 0.0) + jnp.where(cell + 1 == point, frac, 0.0)
    low, high = [], []
    for y in range(ROWS):
        t = (y + 0.5) / ROWS
        low.append((1.0 - t) * table)
        high.append(t * table)
    both = jnp.concatenate([jnp.concatenate(low, axis=1), jnp.concatenate(high, axis=1)], axis=0)
    for k in range(members):
        rows = coarse_ref[pl.ds(k, 2 * points, stride=members), :]
        product = lax.dot_general(
            rows, both, (((0,), (0,)), ((), ())),
            precision=lax.Precision.HIGHEST, preferred_element_type=jnp.float32)
        weights_ref[k] = product.reshape(weights_ref.shape[1:])


def analysis_kernel(members, block, coarse_ref, cell_ref, frac_ref, sources_ref, first_ref, last_ref, weights_ref, wide_ref):
    sources = sources_ref.shape[0] // FIELDS
    nlon = cell_ref.shape[1]
    half = ROWS * LEV // 2
    make_weights(coarse_ref, cell_ref, frac_ref, weights_ref, members)
    wide_ref[...] = sources_ref[...].astype(jnp.float32)
    upper = lax.broadcasted_iota(jnp.int32, (half, nlon), 0) < LEV
    for pair, out_ref in enumerate((first_ref, last_ref)):
        lanes = [slice(y * nlon, (y + 1) * nlon) for y in (2 * pair, 2 * pair + 1)]

        def some_members(b, carry, pair=pair, out_ref=out_ref, lanes=lanes):
            totals = [[None] * FIELDS for _ in range(block)]
            for s in range(sources):
                fields = [wide_ref[s * FIELDS + f, pair * half:(pair + 1) * half, :] for f in range(FIELDS)]
                for j in range(block):
                    row = weights_ref.at[b * block + j, s // 8]
                    w = jnp.where(
                        upper,
                        jnp.broadcast_to(row[s % 8:s % 8 + 1, lanes[0]], (half, nlon)),
                        jnp.broadcast_to(row[s % 8:s % 8 + 1, lanes[1]], (half, nlon)))
                    for f in range(FIELDS):
                        term = w * fields[f]
                        totals[j][f] = term if s == 0 else totals[j][f] + term
            for j in range(block):
                for f in range(FIELDS):
                    out_ref[(b * block + j) * FIELDS + f] = totals[j][f]
            return carry

        lax.fori_loop(0, members // block, some_members, 0)


def analyse(coarse, cell, frac, sources, members):
    nlon = cell.shape[1]
    count = sources.shape[0] // FIELDS
    pair = jax.ShapeDtypeStruct((members * FIELDS, ROWS * LEV // 2, nlon), jnp.float32)
    return pl.pallas_call(
        functools.partial(analysis_kernel, members, 4),
        out_shape=(pair, pair),
        in_specs=[VMEM] * 4,
        out_specs=(VMEM, VMEM),
        scratch_shapes=[
            pltpu.VMEM((members, count // 8, 8, ROWS * nlon), jnp.float32),
            pltpu.VMEM(sources.shape, jnp.float32),
        ],
        compiler_params=pltpu.CompilerParams(vmem_limit_bytes=VMEM_LIMIT),
        name="analysis",
    )(coarse, cell, frac, sources)


def forecast_kernel(edges_ref, viscosity_ref, first_ref, last_ref, before_ref, after_ref, out_ref):
    half, nlon = first_ref.shape[1:]
    members = first_ref.shape[0] // FIELDS
    upper = lax.broadcasted_iota(jnp.int32, (half, nlon), 0) < LEV
    spread = 0.25 * jnp.concatenate([viscosity_ref[...]] * 2, axis=0)
    stay = 1.0 - 4.0 * spread
    keep = jnp.where(upper, edges_ref[1], edges_ref[0]) != 0

    def swap(a):
        return pltpu.roll(a, LEV, 0)

    def advance(centre, north, south):
        west = [pltpu.roll(a, 1, 1) for a in centre]
        east = [pltpu.roll(a, nlon - 1, 1) for a in centre]
        dx = [e - w for e, w in zip(east, west)]
        dy = [n - s for n, s in zip(north, south)]
        u, v = centre[0] * -0.125, centre[1] * -0.125
        out = []
        for f in range(FIELDS):
            around = (east[f] + west[f]) + (north[f] + south[f])
            out.append(stay * centre[f] + spread * around + (u * dx[f] + v * dy[f]))
        out[0] = out[0] - 0.125 * dx[2]
        out[1] = out[1] - 0.125 * dy[2]
        out[2] = out[2] - 0.125 * (dx[0] + dy[1])
        return out

    def one_member(k, carry):
        base = k * FIELDS
        fields = range(FIELDS)
        first = [first_ref[base + f] for f in fields]
        last = [last_ref[base + f] for f in fields]
        before = [before_ref[base + f] for f in fields]
        after = [after_ref[base + f] for f in fields]
        edge = [jnp.where(upper, after[f], before[f]) for f in fields]
        sf, sl = [swap(a) for a in first], [swap(a) for a in last]
        sb, sa = [swap(a) for a in before], [swap(a) for a in after]

        def mix(a, b):
            return [jnp.where(upper, x, y) for x, y in zip(a, b)]

        first1 = advance(first, mix(sf, sl), mix(sb, sf))
        last1 = advance(last, mix(sl, sa), mix(sf, sl))
        edge1 = advance(edge, mix(sa, sf), mix(sl, sb))
        edge1 = [jnp.where(keep, a, 0.0) for a in edge1]
        sf, sl, se = [swap(a) for a in first1], [swap(a) for a in last1], [swap(a) for a in edge1]
        first2 = advance(first1, mix(sf, sl), mix(se, sf))
        last2 = advance(last1, mix(sl, se), mix(sf, sl))
        for f in fields:
            out_ref[base + f, :half, :] = first2[f]
            out_ref[base + f, half:, :] = last2[f]
        return carry

    lax.fori_loop(0, members, one_member, 0)


def forecast(edges, viscosity, first, last, before, after):
    count, half, nlon = first.shape
    return pl.pallas_call(
        forecast_kernel,
        out_shape=jax.ShapeDtypeStruct((count, 2 * half, nlon), jnp.float32),
        in_specs=[SMEM] + [VMEM] * 5,
        out_specs=VMEM,
        compiler_params=pltpu.CompilerParams(vmem_limit_bytes=VMEM_LIMIT),
        name="forecast",
    )(edges, viscosity, first, last, before, after)


def on_device(states, src_ids, coarse_w, lon_cell, lon_frac, viscosity):
    members, fields, rows, lev, nlon = states.shape
    picked = pick(states.reshape(members, fields, rows * lev, nlon), src_ids)
    sources = lax.all_gather(picked, "mem")
    sources = sources.reshape(-1, rows * lev, nlon)
    coarse = jnp.swapaxes(coarse_w, 2, 3)
    coarse = coarse.reshape(-1, coarse.shape[3])
    first, last = analyse(coarse, lon_cell[None], lon_frac[None], sources, members)
    size = lax.axis_size("lat")
    up = [(i, i + 1) for i in range(size - 1)]
    down = [(i + 1, i) for i in range(size - 1)]
    before = lax.ppermute(last, "lat", up)
    after = lax.ppermute(first, "lat", down)
    place = lax.axis_index("lat")
    edges = jnp.stack([place != 0, place != size - 1]).astype(jnp.int32)
    out = forecast(edges, viscosity, first, last, before, after)
    return out.reshape(members, fields, rows, lev, nlon)


def solution(mesh):
    in_specs = (
        P("mem", None, "lat", None, None),
        P("mem", None),
        P("lat", None, None, "mem"),
        P(),
        P(),
        P(),
    )
    out_specs = P("mem", None, "lat", None, None)
    return jax.shard_map(
        on_device, mesh=mesh, in_specs=in_specs, out_specs=out_specs, check_vma=False
    )
```

time: 184 us -> 73.8 us (0.40)
  the two profiles are of different devices: /device:TPU:64 before, /device:TPU:192 now
where the time goes in v1:
time: 73.8 us; the launch traced here: 73.7 us
  blocking collectives  41.1 us (56%)
  Pallas kernels  13.9 us (19%)
  waiting for transfers between devices  10.6 us (14%)
  starting transfers between devices  7.3 us (10%)
    all_gather x1, blocking collectives, on_device(): sources = lax.all_gather(picked, 'mem')  41.1 us
    ppermute x1, waiting for transfers between devices, on_device(): before = lax.ppermute(last, 'lat', up)  8.04 us
    pallas_call x1, Pallas kernels, pick(): pl.pallas_call(pick_kernel, out_shape=jax.ShapeDtypeStruct((n,) + states....  6.8 us
    ppermute x1, starting transfers between devices, on_device(): after = lax.ppermute(first, 'lat', down)  5.38 us
    pallas_call x1, Pallas kernels, forecast(): pl.pallas_call(forecast_kernel, out_shape=jax.ShapeDtypeStruct((count, 2...  4.3 us
    pallas_call x1, Pallas kernels, analyse(): pl.pallas_call(functools.partial(analysis_kernel, members, 4), out_shape=...  2.81 us
    ppermute x1, waiting for transfers between devices, on_device(): after = lax.ppermute(first, 'lat', down)  2.55 us
    ppermute x1, starting transfers between devices, on_device(): before = lax.ppermute(last, 'lat', up)  1.92 us
  transfers between devices with their start and end apart: 2, of which 2 were waited for; matrix products, arithmetic and copies ran while one was open for 0% of the time, Pallas kernels for 0%

profile of v1, /device:TPU:192, one launch (start us, length us, event | category | flops | bytes accessed | tf_op | source)
XLA Modules:
  0.0 73.7 jit_solution(17040443572873110301)
XLA Ops:
  0.0 6.8 %pick.1 = bf16[8,5,16,128]{3,2,1,0:T(8,128)(2,1)} custom-call(s32[1,8]{1,0:T(1,128)} %ids_ref.1, bf16[16,5,16,128]{3,2,1,0:T(8,128)(2,1)} %bitcast.14), custom_call_target="tpu_custom_call" | custom-call | tf_op jit(solution)/shard_map/pick/pallas_call | solution.py:31
  6.8 0.0 copy-start
  6.8 41.1 %all-gather = bf16[32,5,16,128]{3,2,1,0:T(8,128)(2,1)S(1)} all-gather(bf16[8,5,16,128]{3,2,1,0:T(8,128)(2,1)} %pick.1), channel_id=2, replica_groups=mesh['mem'=4,'lat'=256] {'mem'}, dimensions={0}, use_global_device_ids=true | all-gather | bytes 819200 | tf_op jit(solution)/shard_map/all_gather | solution.py:181
  47.9 0.0 copy-start.2
  47.9 0.0 copy-start.3
  47.9 0.0 copy-done
  47.9 0.6 copy-done.2
  48.5 0.0 copy-done.3
  48.6 2.8 %analysis.1 = (f32[80,8,128]{2,1,0:T(8,128)S(1)}, f32[80,8,128]{2,1,0:T(8,128)S(1)}) custom-call(f32[512,32]{1,0:T(8,128)S(1)} %bitcast.11, s32[1,128]{1,0:T(1,128)S(1)} %bitcast.12, f32[1,128]{1,0:T(1,128)S(1)} %bitcast.13, bf16[160,16,128]{2,1,0:T(8,128)(2,1)S(1)} %bitcast.10), custom_call_target="tpu_custom_call" | custom-call | tf_op jit(solution)/shard_map/analysis/pallas_call | solution.py:97
  51.4 5.4 %collective-permute-start.1 = (f32[80,8,128]{2,1,0:T(8,128)S(1)}, f32[80,8,128]{2,1,0:T(8,128)S(1)}, u32[]{:S(2)}, u32[]{:S(2)}) collective-permute-start(f32[80,8,128]{2,1,0:T(8,128)S(1)} %get-tuple-element.7.first_ref), channel_id=1, source_target_pairs={{1,0},{2,1},{3,2},{4,3},{5,4},{6,5},{7,6},{8,7},{9,8},{10,9},{11,1... | collective-permute-start | bytes 983048 | tf_op jit(solution)/shard_map/ppermute | solution.py:190
  56.8 1.9 %collective-permute-start = (f32[80,8,128]{2,1,0:T(8,128)S(1)}, f32[80,8,128]{2,1,0:T(8,128)S(1)}, u32[]{:S(2)}, u32[]{:S(2)}) collective-permute-start(f32[80,8,128]{2,1,0:T(8,128)S(1)} %get-tuple-element.8.last_ref), channel_id=1, source_target_pairs={{0,1},{1,2},{2,3},{3,4},{4,5},{5,6},{6,7},{7,8},{8,9},{9,10},{10,1... | collective-permute-start | bytes 983048 | tf_op jit(solution)/shard_map/ppermute | solution.py:189
  58.7 0.0 copy-start.1
  58.7 0.1 add_convert_fusion.edges_ref
  58.8 2.5 %collective-permute-done.1.after_ref = f32[80,8,128]{2,1,0:T(8,128)S(1)} collective-permute-done((f32[80,8,128]{2,1,0:T(8,128)S(1)}, f32[80,8,128]{2,1,0:T(8,128)S(1)}, u32[]{:S(2)}, u32[]{:S(2)}) %collective-permute-start.1) | collective-permute-done | bytes 327712 | tf_op jit(solution)/shard_map/ppermute | solution.py:190
  61.3 8.0 %collective-permute-done.before_ref = f32[80,8,128]{2,1,0:T(8,128)S(1)} collective-permute-done((f32[80,8,128]{2,1,0:T(8,128)S(1)}, f32[80,8,128]{2,1,0:T(8,128)S(1)}, u32[]{:S(2)}, u32[]{:S(2)}) %collective-permute-start) | collective-permute-done | bytes 327712 | tf_op jit(solution)/shard_map/ppermute | solution.py:189
  69.4 0.0 copy-done.1
  69.4 4.3 %forecast.1 = f32[80,16,128]{2,1,0:T(8,128)} custom-call(s32[2]{0:T(128)S(1)} %add_convert_fusion.edges_ref, f32[4,128]{1,0:T(4,128)S(1)} %copy-done.1, f32[80,8,128]{2,1,0:T(8,128)S(1)} %get-tuple-element.7.first_ref, f32[80,8,128]{2,1,0:T(8,128)S(1)} %get-tuple-element.8.last_ref, f32[80,8,128]{2,1,0:T(8,128)S(1)} %collective-permute-done.before_ref, ...), custom_call_target="tpu_custom_call" | custom-call | tf_op jit(solution)/shard_map/forecast/pallas_call | solution.py:168
Async XLA Ops:
  6.8 41.1 %copy-start = (f32[2,16,32,16]{2,3,1,0:T(8,128)S(1)}, f32[2,16,32,16]{2,3,1,0:T(8,128)}, u32[]{:S(2)}) copy-start(f32[2,16,32,16]{2,3,1,0:T(8,128)} %param.8) | copy-start | bytes 196612
  47.9 0.7 copy-start.2
  47.9 0.7 copy-start.3
  51.4 10.0 %collective-permute-start.1 = (f32[80,8,128]{2,1,0:T(8,128)S(1)}, f32[80,8,128]{2,1,0:T(8,128)S(1)}, u32[]{:S(2)}, u32[]{:S(2)}) collective-permute-start(f32[80,8,128]{2,1,0:T(8,128)S(1)} %get-tuple-element.7.first_ref), channel_id=1, source_target_pairs={{1,0},{2,1},{3,2},{4,3},{5,4},{6,5},{7,6},{8,7},{9,8},{10,9},{11,1... | collective-permute-start | bytes 983048 | tf_op jit(solution)/shard_map/ppermute | solution.py:190
  56.8 12.6 %collective-permute-start = (f32[80,8,128]{2,1,0:T(8,128)S(1)}, f32[80,8,128]{2,1,0:T(8,128)S(1)}, u32[]{:S(2)}, u32[]{:S(2)}) collective-permute-start(f32[80,8,128]{2,1,0:T(8,128)S(1)} %get-tuple-element.8.last_ref), channel_id=1, source_target_pairs={{0,1},{1,2},{2,3},{3,4},{4,5},{5,6},{6,7},{7,8},{8,9},{9,10},{10,1... | collective-permute-start | bytes 983048 | tf_op jit(solution)/shard_map/ppermute | solution.py:189
  58.7 10.7 %copy-start.1 = (f32[4,128]{1,0:T(4,128)S(1)}, f32[4,128]{1,0:T(4,128)}, u32[]{:S(2)}) copy-start(f32[4,128]{1,0:T(4,128)} %viscosity_ref.1) | copy-start | bytes 6148

commit v2 on v1

v2 whole, which is shorter than its diff:
```python
import functools

import jax
import jax.numpy as jnp
from jax import lax
from jax.experimental import pallas as pl
from jax.experimental.pallas import tpu as pltpu
from jax.sharding import PartitionSpec as P

ROWS = 4
LEV = 4
FIELDS = 5
GROUP = 2
PARTS = 4
VMEM_LIMIT = 48 * 1024 * 1024
VMEM = pl.BlockSpec(memory_space=pltpu.VMEM)
SMEM = pl.BlockSpec(memory_space=pltpu.SMEM)


def pick_kernel(ids_ref, states_ref, out_ref):
    for i in range(out_ref.shape[0]):
        out_ref[i] = states_ref[ids_ref[0, i]]


def pick(states, src_ids):
    return pl.pallas_call(
        pick_kernel,
        out_shape=jax.ShapeDtypeStruct((src_ids.shape[1],) + states.shape[1:], states.dtype),
        in_specs=[SMEM, VMEM],
        out_specs=VMEM,
        name="pick",
    )(src_ids, states)


def make_weights(pair, coarse_ref, cell_ref, frac_ref, weights_ref):
    members = weights_ref.shape[0]
    nlon = cell_ref.shape[1]
    points = coarse_ref.shape[0] // (2 * members)
    point = lax.broadcasted_iota(jnp.int32, (points, nlon), 0)
    cell = jnp.broadcast_to(cell_ref[...], (points, nlon))
    frac = jnp.broadcast_to(frac_ref[...], (points, nlon))
    table = jnp.where(cell == point, 1.0 - frac, 0.0) + jnp.where(cell + 1 == point, frac, 0.0)
    low, high = [], []
    for i in range(2):
        t = ((2 * pair + i).astype(jnp.float32) + 0.5) / ROWS
        low.append((1.0 - t) * table)
        high.append(t * table)
    both = jnp.concatenate([jnp.concatenate(low, axis=1), jnp.concatenate(high, axis=1)], axis=0)
    for k in range(members):
        rows = coarse_ref[pl.ds(k, 2 * points, stride=members), :]
        product = lax.dot_general(
            rows, both, (((0,), (0,)), ((), ())),
            precision=lax.Precision.HIGHEST, preferred_element_type=jnp.float32)
        weights_ref[k] = product.reshape(weights_ref.shape[1:])


def analysis_kernel(facing, block, *refs):
    odd_ref, coarse_ref, cell_ref, frac_ref, sources_ref, *out_refs = refs[:-2]
    weights_ref, wide_ref = refs[-2:]
    pair = odd_ref[0] if facing else 1 - odd_ref[0]
    count = sources_ref.shape[0]
    sources = count // FIELDS
    members = weights_ref.shape[0]
    half, nlon = out_refs[0].shape[1:]
    make_weights(pair, coarse_ref, cell_ref, frac_ref, weights_ref)
    upper = lax.broadcasted_iota(jnp.int32, (half, nlon), 0) < LEV
    later = jnp.full((half, nlon), pair, jnp.int32) != 0
    for i in range(count):
        whole = sources_ref[i].astype(jnp.float32)
        wide_ref[i] = jnp.where(later, whole[half:], whole[:half])
    share = members // len(out_refs)

    def some_members(b, carry, start, out_ref):
        totals = [[None] * FIELDS for _ in range(block)]
        for s in range(sources):
            fields = [wide_ref[s * FIELDS + f] for f in range(FIELDS)]
            for j in range(block):
                row = weights_ref.at[start + b * block + j, s // 8]
                low, high = [
                    jnp.broadcast_to(row[s % 8:s % 8 + 1, i * nlon:(i + 1) * nlon], (half, nlon)) for i in range(2)
                ]
                w = jnp.where(upper, low, high)
                for f in range(FIELDS):
                    term = w * fields[f]
                    totals[j][f] = term if s == 0 else totals[j][f] + term
        for j in range(block):
            for f in range(FIELDS):
                out_ref[(b * block + j) * FIELDS + f] = totals[j][f]
        return carry

    for i, out_ref in enumerate(out_refs):
        lax.fori_loop(0, share // block, functools.partial(some_members, start=i * share, out_ref=out_ref), 0)


def analyse(facing, pieces, odd, coarse, cell, frac, sources, members):
    nlon = cell.shape[1]
    half = ROWS * LEV // 2
    count = sources.shape[0]
    return pl.pallas_call(
        functools.partial(analysis_kernel, facing, 4),
        out_shape=[jax.ShapeDtypeStruct((members * FIELDS // pieces, half, nlon), jnp.float32)] * pieces,
        in_specs=[SMEM] + [VMEM] * 4,
        out_specs=[VMEM] * pieces,
        scratch_shapes=[
            pltpu.VMEM((members, count // FIELDS // 8, 8, 2 * nlon), jnp.float32),
            pltpu.VMEM((count, half, nlon), jnp.float32),
        ],
        compiler_params=pltpu.CompilerParams(vmem_limit_bytes=VMEM_LIMIT),
        cost_estimate=pl.CostEstimate(flops=2 * 10**10, bytes_accessed=2 * 10**7, transcendentals=0),
        name="analysis_outer" if facing else "analysis_inner",
    )(odd, coarse, cell, frac, sources)


def forecast_kernel(
    group, place_ref, viscosity_ref, inside_low_ref, inside_high_ref, outside_ref, inner_low_ref, inner_high_ref, outer_ref,
    out_ref, result_ref, sem
):
    half, nlon = outer_ref.shape[1:]
    count = outer_ref.shape[0]
    members = count // FIELDS
    upper = lax.broadcasted_iota(jnp.int32, (half, nlon), 0) < LEV
    spread = 0.25 * jnp.concatenate([viscosity_ref[...]] * 2, axis=0)
    stay = 1.0 - 4.0 * spread
    keep = jnp.where(upper, place_ref[1], place_ref[0]) != 0
    odd = jnp.full((half, nlon), place_ref[2], jnp.int32) != 0

    def swap(a):
        return pltpu.roll(a, LEV, 0)

    def advance(centre, north, south):
        west = [pltpu.roll(a, 1, 1) for a in centre]
        east = [pltpu.roll(a, nlon - 1, 1) for a in centre]
        dx = [e - w for e, w in zip(east, west)]
        dy = [n - s for n, s in zip(north, south)]
        u, v = centre[0] * -0.125, centre[1] * -0.125
        out = []
        for f in range(FIELDS):
            around = (east[f] + west[f]) + (north[f] + south[f])
            out.append(stay * centre[f] + spread * around + (u * dx[f] + v * dy[f]))
        out[0] = out[0] - 0.125 * dx[2]
        out[1] = out[1] - 0.125 * dy[2]
        out[2] = out[2] - 0.125 * (dx[0] + dy[1])
        return out

    def mix(a, b):
        return [jnp.where(upper, x, y) for x, y in zip(a, b)]

    def one_member(k, high):
        base = k * FIELDS
        near = base - (count // 2 if high else 0)
        inner_ref, inside_ref = (inner_high_ref, inside_high_ref) if high else (inner_low_ref, inside_low_ref)
        fields = range(FIELDS)
        outer = [outer_ref[base + f] for f in fields]
        inner = [inner_ref[near + f] for f in fields]
        outside = [outside_ref[base + f] for f in fields]
        inside = [inside_ref[near + f] for f in fields]
        first = [jnp.where(odd, inner[f], outer[f]) for f in fields]
        last = [jnp.where(odd, outer[f], inner[f]) for f in fields]
        before = [jnp.where(odd, inside[f], outside[f]) for f in fields]
        after = [jnp.where(odd, outside[f], inside[f]) for f in fields]
        edge = mix(after, before)
        sf, sl = [swap(a) for a in first], [swap(a) for a in last]
        sb, sa = [swap(a) for a in before], [swap(a) for a in after]
        first1 = advance(first, mix(sf, sl), mix(sb, sf))
        last1 = advance(last, mix(sl, sa), mix(sf, sl))
        edge1 = advance(edge, mix(sa, sf), mix(sl, sb))
        edge1 = [jnp.where(keep, a, 0.0) for a in edge1]
        sf, sl, se = [swap(a) for a in first1], [swap(a) for a in last1], [swap(a) for a in edge1]
        first2 = advance(first1, mix(sf, sl), mix(se, sf))
        last2 = advance(last1, mix(sl, se), mix(sf, sl))
        for f in fields:
            result_ref[base + f, :half, :] = first2[f]
            result_ref[base + f, half:, :] = last2[f]

    parts = sem.shape[0]
    copies = []
    for part in range(parts):
        def some(i, carry, part=part):
            for j in range(group):
                one_member(part * (members // parts) + i * group + j, part >= parts // 2)
            return carry

        lax.fori_loop(0, members // parts // group, some, 0)
        rows = pl.ds(part * (count // parts), count // parts)
        copy = pltpu.make_async_copy(result_ref.at[rows], out_ref.at[rows], sem.at[part])
        copy.start()
        copies.append(copy)
    for copy in copies:
        copy.wait()


def forecast(place, viscosity, inside, outside, inner, outer, group=GROUP, parts=PARTS):
    count, half, nlon = outer.shape
    return pl.pallas_call(
        functools.partial(forecast_kernel, group),
        out_shape=jax.ShapeDtypeStruct((count, 2 * half, nlon), jnp.float32),
        in_specs=[SMEM] + [VMEM] * 7,
        out_specs=pl.BlockSpec(memory_space=pl.ANY),
        scratch_shapes=[pltpu.VMEM((count, 2 * half, nlon), jnp.float32), pltpu.SemaphoreType.DMA((parts,))],
        compiler_params=pltpu.CompilerParams(vmem_limit_bytes=VMEM_LIMIT),
        name="forecast",
    )(place, viscosity, *inside, outside, *inner, outer)


def on_device(states, src_ids, coarse_w, lon_cell, lon_frac, viscosity):
    members, fields, rows, lev, nlon = states.shape
    size = lax.axis_size("lat")
    lat = lax.axis_index("lat")
    place = jnp.stack([lat != 0, lat != size - 1, lat % 2 != 0]).astype(jnp.int32)
    odd = place[2:]
    coarse = jnp.swapaxes(coarse_w, 2, 3)
    coarse = coarse.reshape(-1, coarse.shape[3])
    cell, frac = lon_cell[None], lon_frac[None]
    picked = pick(states.reshape(members, fields, rows * lev, nlon), src_ids)
    sources = lax.all_gather(picked, "mem")
    sources = sources.reshape(-1, rows * lev, nlon)
    across = [(i, i + 1) for i in range(1, size - 1, 2)]
    across += [(j, i) for i, j in across]
    within = [(i, i + 1) for i in range(0, size, 2)]
    within += [(j, i) for i, j in within]
    outer, = analyse(True, 1, odd, coarse, cell, frac, sources, members)
    outside = lax.ppermute(outer, "lat", across)
    inner = analyse(False, 2, odd, coarse, cell, frac, sources, members)
    inside = [lax.ppermute(a, "lat", within) for a in inner]
    out = forecast(place, viscosity, inside, outside, inner, outer)
    return out.reshape(members, fields, rows, lev, nlon)


def solution(mesh):
    in_specs = (
        P("mem", None, "lat", None, None),
        P("mem", None),
        P("lat", None, None, "mem"),
        P(),
        P(),
        P(),
    )
    out_specs = P("mem", None, "lat", None, None)
    return jax.shard_map(
        on_device, mesh=mesh, in_specs=in_specs, out_specs=out_specs, check_vma=False
    )
```

time: 73.8 us -> 62.6 us (0.85)
  the two profiles are of different devices: /device:TPU:192 before, /device:TPU:193 now
where the time goes in v2:
time: 62.6 us; the launch traced here: 62.4 us
  blocking collectives  41.2 us (66%)
  starting transfers between devices  9.69 us (15%)
  Pallas kernels  8.72 us (14%)
  waiting for transfers between devices  1.36 us (2%)
  local copies, waits for them, and re-layouts  1.25 us (2%)
    all_gather x1, blocking collectives, on_device(): sources = lax.all_gather(picked, 'mem')  41.2 us
    ppermute x2, starting transfers between devices, on_device(): inside = [lax.ppermute(a, 'lat', within) for a in inner]  6.25 us
    pallas_call x2, Pallas kernels, analyse(): pl.pallas_call(functools.partial(analysis_kernel, facing, 4), out_shape=[...  4.14 us
    ppermute x1, starting transfers between devices, on_device(): outside = lax.ppermute(outer, 'lat', across)  3.44 us
    pallas_call x1, Pallas kernels, forecast(): pl.pallas_call(functools.partial(forecast_kernel, group), out_shape=jax.S...  2.92 us
    pallas_call x1, Pallas kernels, pick(): pl.pallas_call(pick_kernel, out_shape=jax.ShapeDtypeStruct((src_ids.shape...  1.66 us
    ppermute x2, waiting for transfers between devices, on_device(): inside = [lax.ppermute(a, 'lat', within) for a in inner]  1.35 us
  transfers between devices with their start and end apart: 3, of which 1 were waited for; matrix products, arithmetic and copies ran while one was open for 0% of the time, Pallas kernels for 3%

profile of v2, /device:TPU:193, one launch (start us, length us, event | category | flops | bytes accessed | tf_op | source)
XLA Modules:
  0.0 62.4 jit_solution(7685987735760055227)
XLA Ops:
  0.0 0.1 add_convert_fusion.place_ref
  0.1 0.6 slice.3.refs_0_
  0.7 1.7 %pick.1 = bf16[8,5,16,128]{3,2,1,0:T(8,128)(2,1)} custom-call(s32[1,8]{1,0:T(1,128)} %ids_ref.1, bf16[16,5,16,128]{3,2,1,0:T(8,128)(2,1)} %bitcast.19), custom_call_target="tpu_custom_call" | custom-call | tf_op jit(solution)/shard_map/pick/pallas_call | solution.py:26
  2.3 0.0 copy-start.1
  2.3 41.2 %all-gather = bf16[32,5,16,128]{3,2,1,0:T(8,128)(2,1)S(1)} all-gather(bf16[8,5,16,128]{3,2,1,0:T(8,128)(2,1)} %pick.1), channel_id=2, replica_groups=mesh['mem'=4,'lat'=256] {'mem'}, dimensions={0}, use_global_device_ids=true | all-gather | bytes 819200 | tf_op jit(solution)/shard_map/all_gather | solution.py:215
  43.6 0.0 copy-start.2
  43.6 0.0 copy-start.3
  43.6 0.0 copy-done.1
  43.6 0.6 %copy-done.2 = s32[128]{0:T(128)S(1)} copy-done((s32[128]{0:T(128)S(1)}, s32[128]{0:T(128)}, u32[]{:S(2)}) %copy-start.2) | copy-done | bytes 536
  44.2 0.0 copy-done.3
  44.2 2.1 %analysis_outer.1.outer_ref = f32[80,8,128]{2,1,0:T(8,128)S(1)} custom-call(s32[1]{0:T(128)} %slice.3.refs_0_, f32[512,32]{1,0:T(8,128)S(1)} %bitcast.13, s32[1,128]{1,0:T(1,128)S(1)} %bitcast.15, f32[1,128]{1,0:T(1,128)S(1)} %bitcast.17, bf16[160,16,128]{2,1,0:T(8,128)(2,1)S(1)} %bitcast.11), custom_call_target="tpu_custom_call" | custom-call | flops 20000000000 | bytes 20000000 | tf_op jit(solution)/shard_map/analysis_outer/pallas_call | solution.py:99
  46.3 3.4 %collective-permute-start.2 = (f32[80,8,128]{2,1,0:T(8,128)S(1)}, f32[80,8,128]{2,1,0:T(8,128)S(1)}, u32[]{:S(2)}, u32[]{:S(2)}) collective-permute-start(f32[80,8,128]{2,1,0:T(8,128)S(1)} %analysis_outer.1.outer_ref), channel_id=1, source_target_pairs={{1,2},{3,4},{5,6},{7,8},{9,10},{11,12},{13,14},{15,16},{17,18},{19... | collective-permute-start | bytes 983048 | tf_op jit(solution)/shard_map/ppermute | solution.py:222
  49.8 2.1 %analysis_inner.1 = (f32[40,8,128]{2,1,0:T(8,128)S(1)}, f32[40,8,128]{2,1,0:T(8,128)S(1)}) custom-call(s32[1]{0:T(128)} %slice.3.refs_0_, f32[512,32]{1,0:T(8,128)S(1)} %bitcast.14, s32[1,128]{1,0:T(1,128)S(1)} %bitcast.16, f32[1,128]{1,0:T(1,128)S(1)} %bitcast.18, bf16[160,16,128]{2,1,0:T(8,128)(2,1)S(1)} %bitcast.12), custom_call_target="tpu_custom_call" | custom-call | flops 20000000000 | bytes 20000000 | tf_op jit(solution)/shard_map/analysis_inner/pallas_call | solution.py:99
  51.8 0.0 copy-start
  51.8 4.3 %collective-permute-start = (f32[40,8,128]{2,1,0:T(8,128)S(1)}, f32[40,8,128]{2,1,0:T(8,128)S(1)}, u32[]{:S(2)}, u32[]{:S(2)}) collective-permute-start(f32[40,8,128]{2,1,0:T(8,128)S(1)} %get-tuple-element.7.inner_low_ref), channel_id=1, source_target_pairs={{0,1},{2,3},{4,5},{6,7},{8,9},{10,11},{12,13},{14,15},{16,17},{18,... | collective-permute-start | bytes 491528 | tf_op jit(solution)/shard_map/ppermute | solution.py:224
  56.2 1.9 %collective-permute-start.1 = (f32[40,8,128]{2,1,0:T(8,128)S(1)}, f32[40,8,128]{2,1,0:T(8,128)S(1)}, u32[]{:S(2)}, u32[]{:S(2)}) collective-permute-start(f32[40,8,128]{2,1,0:T(8,128)S(1)} %get-tuple-element.8.inner_high_ref), channel_id=1, source_target_pairs={{0,1},{2,3},{4,5},{6,7},{8,9},{10,11},{12,13},{14,15},{16,17},{18,... | collective-permute-start | bytes 491528 | tf_op jit(solution)/shard_map/ppermute | solution.py:224
  58.1 0.0 collective-permute-done.inside_low_ref
  58.1 1.4 %collective-permute-done.1.inside_high_ref = f32[40,8,128]{2,1,0:T(8,128)S(1)} collective-permute-done((f32[40,8,128]{2,1,0:T(8,128)S(1)}, f32[40,8,128]{2,1,0:T(8,128)S(1)}, u32[]{:S(2)}, u32[]{:S(2)}) %collective-permute-start.1) | collective-permute-done | bytes 163872 | tf_op jit(solution)/shard_map/ppermute | solution.py:224
  59.5 0.0 collective-permute-done.2.outside_ref
  59.5 0.0 copy-done
  59.5 2.9 %forecast.1 = f32[80,16,128]{2,1,0:T(8,128)} custom-call(s32[3]{0:T(128)S(1)} %add_convert_fusion.place_ref, f32[4,128]{1,0:T(4,128)S(1)} %copy-done, f32[40,8,128]{2,1,0:T(8,128)S(1)} %collective-permute-done.inside_low_ref, f32[40,8,128]{2,1,0:T(8,128)S(1)} %collective-permute-done.1.inside_high_ref, f32[80,8,128]{2,1,0:T(8,128)S(1)} %collective-permute-done.2.outside_ref, ...), custom_call_target="tpu_custom_call" | custom-call | tf_op jit(solution)/shard_map/forecast/pallas_call | solution.py:194
Async XLA Ops:
  2.3 41.2 %copy-start.1 = (f32[2,16,32,16]{2,3,1,0:T(8,128)S(1)}, f32[2,16,32,16]{2,3,1,0:T(8,128)}, u32[]{:S(2)}) copy-start(f32[2,16,32,16]{2,3,1,0:T(8,128)} %param.8) | copy-start | bytes 196612
  43.6 0.7 %copy-start.2 = (s32[128]{0:T(128)S(1)}, s32[128]{0:T(128)}, u32[]{:S(2)}) copy-start(s32[128]{0:T(128)} %param.9) | copy-start | bytes 1540
  43.6 0.7 %copy-start.3 = (f32[128]{0:T(128)S(1)}, f32[128]{0:T(128)}, u32[]{:S(2)}) copy-start(f32[128]{0:T(128)} %param.10) | copy-start | bytes 1540
  46.3 13.2 %collective-permute-start.2 = (f32[80,8,128]{2,1,0:T(8,128)S(1)}, f32[80,8,128]{2,1,0:T(8,128)S(1)}, u32[]{:S(2)}, u32[]{:S(2)}) collective-permute-start(f32[80,8,128]{2,1,0:T(8,128)S(1)} %analysis_outer.1.outer_ref), channel_id=1, source_target_pairs={{1,2},{3,4},{5,6},{7,8},{9,10},{11,12},{13,14},{15,16},{17,18},{19... | collective-permute-start | bytes 983048 | tf_op jit(solution)/shard_map/ppermute | solution.py:222
  51.8 7.6 %copy-start = (f32[4,128]{1,0:T(4,128)S(1)}, f32[4,128]{1,0:T(4,128)}, u32[]{:S(2)}) copy-start(f32[4,128]{1,0:T(4,128)} %viscosity_ref.1) | copy-start | bytes 6148
  51.8 6.3 %collective-permute-start = (f32[40,8,128]{2,1,0:T(8,128)S(1)}, f32[40,8,128]{2,1,0:T(8,128)S(1)}, u32[]{:S(2)}, u32[]{:S(2)}) collective-permute-start(f32[40,8,128]{2,1,0:T(8,128)S(1)} %get-tuple-element.7.inner_low_ref), channel_id=1, source_target_pairs={{0,1},{2,3},{4,5},{6,7},{8,9},{10,11},{12,13},{14,15},{16,17},{18,... | collective-permute-start | bytes 491528 | tf_op jit(solution)/shard_map/ppermute | solution.py:224
  56.2 3.3 %collective-permute-start.1 = (f32[40,8,128]{2,1,0:T(8,128)S(1)}, f32[40,8,128]{2,1,0:T(8,128)S(1)}, u32[]{:S(2)}, u32[]{:S(2)}) collective-permute-start(f32[40,8,128]{2,1,0:T(8,128)S(1)} %get-tuple-element.8.inner_high_ref), channel_id=1, source_target_pairs={{0,1},{2,3},{4,5},{6,7},{8,9},{10,11},{12,13},{14,15},{16,17},{18,... | collective-permute-start | bytes 491528 | tf_op jit(solution)/shard_map/ppermute | solution.py:224

commit v3 on v2

--- a/solution.py
+++ b/solution.py
@@ -11,6 +11,7 @@
 LEV = 4
 FIELDS = 5
 GROUP = 2
+PAD = 1
 PARTS = 4
 VMEM_LIMIT = 48 * 1024 * 1024
 VMEM = pl.BlockSpec(memory_space=pltpu.VMEM)
@@ -55,9 +56,9 @@
 
 
 def analysis_kernel(facing, block, *refs):
-    odd_ref, coarse_ref, cell_ref, frac_ref, sources_ref, *out_refs = refs[:-2]
+    place_ref, coarse_ref, cell_ref, frac_ref, sources_ref, *out_refs = refs[:-2]
     weights_ref, wide_ref = refs[-2:]
-    pair = odd_ref[0] if facing else 1 - odd_ref[0]
+    pair = place_ref[2] if facing else 1 - place_ref[2]
     count = sources_ref.shape[0]
     sources = count // FIELDS
     members = weights_ref.shape[0]
@@ -88,17 +89,19 @@
                 out_ref[(b * block + j) * FIELDS + f] = totals[j][f]
         return carry
 
+    if facing:
+        out_refs[0][members * FIELDS:] = jnp.zeros((PAD, half, nlon), jnp.float32)
     for i, out_ref in enumerate(out_refs):
         lax.fori_loop(0, share // block, functools.partial(some_members, start=i * share, out_ref=out_ref), 0)
 
 
-def analyse(facing, pieces, odd, coarse, cell, frac, sources, members):
+def analyse(facing, pieces, place, coarse, cell, frac, sources, members):
     nlon = cell.shape[1]
     half = ROWS * LEV // 2
     count = sources.shape[0]
     return pl.pallas_call(
         functools.partial(analysis_kernel, facing, 4),
-        out_shape=[jax.ShapeDtypeStruct((members * FIELDS // pieces, half, nlon), jnp.float32)] * pieces,
+        out_shape=[jax.ShapeDtypeStruct((members * FIELDS // pieces + (PAD if facing else 0), half, nlon), jnp.float32)] * pieces,
         in_specs=[SMEM] + [VMEM] * 4,
         out_specs=[VMEM] * pieces,
         scratch_shapes=[
@@ -108,15 +111,13 @@
         compiler_params=pltpu.CompilerParams(vmem_limit_bytes=VMEM_LIMIT),
         cost_estimate=pl.CostEstimate(flops=2 * 10**10, bytes_accessed=2 * 10**7, transcendentals=0),
         name="analysis_outer" if facing else "analysis_inner",
-    )(odd, coarse, cell, frac, sources)
+    )(place, coarse, cell, frac, sources)
 
 
 def forecast_kernel(
-    group, place_ref, viscosity_ref, inside_low_ref, inside_high_ref, outside_ref, inner_low_ref, inner_high_ref, outer_ref,
-    out_ref, result_ref, sem
+    group, place_ref, viscosity_ref, inside_ref, outside_ref, inner_ref, outer_ref, out_ref, result_ref, sem
 ):
-    half, nlon = outer_ref.shape[1:]
-    count = outer_ref.shape[0]
+    count, half, nlon = inner_ref.shape
     members = count // FIELDS
     upper = lax.broadcasted_iota(jnp.int32, (half, nlon), 0) < LEV
     spread = 0.25 * jnp.concatenate([viscosity_ref[...]] * 2, axis=0)
@@ -145,15 +146,13 @@
     def mix(a, b):
         return [jnp.where(upper, x, y) for x, y in zip(a, b)]
 
-    def one_member(k, high):
+    def one_member(k):
         base = k * FIELDS
-        near = base - (count // 2 if high else 0)
-        inner_ref, inside_ref = (inner_high_ref, inside_high_ref) if high else (inner_low_ref, inside_low_ref)
         fields = range(FIELDS)
         outer = [outer_ref[base + f] for f in fields]
-        inner = [inner_ref[near + f] for f in fields]
+        inner = [inner_ref[base + f] for f in fields]
         outside = [outside_ref[base + f] for f in fields]
-        inside = [inside_ref[near + f] for f in fields]
+        inside = [inside_ref[base + f] for f in fields]
         first = [jnp.where(odd, inner[f], outer[f]) for f in fields]
         last = [jnp.where(odd, outer[f], inner[f]) for f in fields]
         before = [jnp.where(odd, inside[f], outside[f]) for f in fields]
@@ -177,7 +176,7 @@
     for part in range(parts):
         def some(i, carry, part=part):
             for j in range(group):
-                one_member(part * (members // parts) + i * group + j, part >= parts // 2)
+                one_member(part * (members // parts) + i * group + j)
             return carry
 
         lax.fori_loop(0, members // parts // group, some, 0)
@@ -190,16 +189,16 @@
 
 
 def forecast(place, viscosity, inside, outside, inner, outer, group=GROUP, parts=PARTS):
-    count, half, nlon = outer.shape
+    count, half, nlon = inner.shape
     return pl.pallas_call(
         functools.partial(forecast_kernel, group),
         out_shape=jax.ShapeDtypeStruct((count, 2 * half, nlon), jnp.float32),
-        in_specs=[SMEM] + [VMEM] * 7,
+        in_specs=[SMEM] + [VMEM] * 5,
         out_specs=pl.BlockSpec(memory_space=pl.ANY),
         scratch_shapes=[pltpu.VMEM((count, 2 * half, nlon), jnp.float32), pltpu.SemaphoreType.DMA((parts,))],
         compiler_params=pltpu.CompilerParams(vmem_limit_bytes=VMEM_LIMIT),
         name="forecast",
-    )(place, viscosity, *inside, outside, *inner, outer)
+    )(place, viscosity, inside, outside, inner, outer)
 
 
 def on_device(states, src_ids, coarse_w, lon_cell, lon_frac, viscosity):
@@ -207,7 +206,6 @@
     size = lax.axis_size("lat")
     lat = lax.axis_index("lat")
     place = jnp.stack([lat != 0, lat != size - 1, lat % 2 != 0]).astype(jnp.int32)
-    odd = place[2:]
     coarse = jnp.swapaxes(coarse_w, 2, 3)
     coarse = coarse.reshape(-1, coarse.shape[3])
     cell, frac = lon_cell[None], lon_frac[None]
@@ -218,10 +216,10 @@
     across += [(j, i) for i, j in across]
     within = [(i, i + 1) for i in range(0, size, 2)]
     within += [(j, i) for i, j in within]
-    outer, = analyse(True, 1, odd, coarse, cell, frac, sources, members)
+    outer, = analyse(True, 1, place, coarse, cell, frac, sources, members)
     outside = lax.ppermute(outer, "lat", across)
-    inner = analyse(False, 2, odd, coarse, cell, frac, sources, members)
-    inside = [lax.ppermute(a, "lat", within) for a in inner]
+    inner, = analyse(False, 1, place, coarse, cell, frac, sources, members)
+    inside = lax.ppermute(inner, "lat", within)
     out = forecast(place, viscosity, inside, outside, inner, outer)
     return out.reshape(members, fields, rows, lev, nlon)
 

time: 62.6 us -> 61.7 us (0.986)
  the two profiles are of different devices: /device:TPU:193 before, /device:TPU:64 now
where the time goes in v3:
time: 61.7 us; the launch traced here: 61.5 us
  blocking collectives  41.4 us (67%)
  Pallas kernels  8.67 us (14%)
  waiting for transfers between devices  6.74 us (11%)
  starting transfers between devices  3.84 us (6%)
  local copies, waits for them, and re-layouts  0.68 us (1%)
    all_gather x1, blocking collectives, on_device(): sources = lax.all_gather(picked, 'mem')  41.4 us
    ppermute x1, waiting for transfers between devices, on_device(): outside = lax.ppermute(outer, 'lat', across)  5.14 us
    pallas_call x2, Pallas kernels, analyse(): pl.pallas_call(functools.partial(analysis_kernel, facing, 4), out_shape=[...  4.11 us
    pallas_call x1, Pallas kernels, forecast(): pl.pallas_call(functools.partial(forecast_kernel, group), out_shape=jax.S...  2.9 us
    ppermute x1, starting transfers between devices, on_device(): outside = lax.ppermute(outer, 'lat', across)  1.92 us
    ppermute x1, starting transfers between devices, on_device(): inside = lax.ppermute(inner, 'lat', within)  1.92 us
    pallas_call x1, Pallas kernels, pick(): pl.pallas_call(pick_kernel, out_shape=jax.ShapeDtypeStruct((src_ids.shape...  1.66 us
    ppermute x1, waiting for transfers between devices, on_device(): inside = lax.ppermute(inner, 'lat', within)  1.59 us
  transfers between devices with their start and end apart: 2, of which 2 were waited for; matrix products, arithmetic and copies ran while one was open for 0% of the time, Pallas kernels for 3%

profile of v3, /device:TPU:64, one launch (start us, length us, event | category | flops | bytes accessed | tf_op | source)
XLA Modules:
  0.0 61.5 jit_solution(15864603279285370628)
XLA Ops:
  0.0 1.7 %pick.1 = bf16[8,5,16,128]{3,2,1,0:T(8,128)(2,1)} custom-call(s32[1,8]{1,0:T(1,128)} %ids_ref.1, bf16[16,5,16,128]{3,2,1,0:T(8,128)(2,1)} %bitcast.19), custom_call_target="tpu_custom_call" | custom-call | tf_op jit(solution)/shard_map/pick/pallas_call | solution.py:27
  1.7 0.0 copy-start.1
  1.7 41.4 %all-gather = bf16[32,5,16,128]{3,2,1,0:T(8,128)(2,1)S(1)} all-gather(bf16[8,5,16,128]{3,2,1,0:T(8,128)(2,1)} %pick.1), channel_id=2, replica_groups=mesh['mem'=4,'lat'=256] {'mem'}, dimensions={0}, use_global_device_ids=true | all-gather | bytes 819200 | tf_op jit(solution)/shard_map/all_gather | solution.py:213
  43.1 0.1 add_convert_fusion.refs_0_.place_ref
  43.2 0.0 copy-start.2
  43.2 0.0 copy-start.3
  43.2 0.0 copy-done.1
  43.2 0.7 %copy-done.2 = s32[128]{0:T(128)S(1)} copy-done((s32[128]{0:T(128)S(1)}, s32[128]{0:T(128)}, u32[]{:S(2)}) %copy-start.2) | copy-done | bytes 536
  43.8 0.0 copy-done.3
  43.9 2.1 %analysis_outer.1.outer_ref = f32[81,8,128]{2,1,0:T(8,128)S(1)} custom-call(s32[3]{0:T(128)S(1)} %add_convert_fusion.refs_0_.place_ref, f32[512,32]{1,0:T(8,128)S(1)} %bitcast.13, s32[1,128]{1,0:T(1,128)S(1)} %bitcast.15, f32[1,128]{1,0:T(1,128)S(1)} %bitcast.17, bf16[160,16,128]{2,1,0:T(8,128)(2,1)S(1)} %bitcast.11), custom_call_target="tpu_custom_call" | custom-call | flops 20000000000 | bytes 20000000 | tf_op jit(solution)/shard_map/analysis_outer/pallas_call | solution.py:102
  45.9 0.0 copy-start
  45.9 1.9 %collective-permute-start.1 = (f32[81,8,128]{2,1,0:T(8,128)S(1)}, f32[81,8,128]{2,1,0:T(8,128)S(1)}, u32[]{:S(2)}, u32[]{:S(2)}) collective-permute-start(f32[81,8,128]{2,1,0:T(8,128)S(1)} %analysis_outer.1.outer_ref), channel_id=1, source_target_pairs={{1,2},{3,4},{5,6},{7,8},{9,10},{11,12},{13,14},{15,16},{17,18},{19... | collective-permute-start | bytes 995336 | tf_op jit(solution)/shard_map/ppermute | solution.py:220
  47.9 2.1 %analysis_inner.1.inner_ref = f32[80,8,128]{2,1,0:T(8,128)S(1)} custom-call(s32[3]{0:T(128)S(1)} %add_convert_fusion.refs_0_.place_ref, f32[512,32]{1,0:T(8,128)S(1)} %bitcast.14, s32[1,128]{1,0:T(1,128)S(1)} %bitcast.16, f32[1,128]{1,0:T(1,128)S(1)} %bitcast.18, bf16[160,16,128]{2,1,0:T(8,128)(2,1)S(1)} %bitcast.12), custom_call_target="tpu_custom_call" | custom-call | flops 20000000000 | bytes 20000000 | tf_op jit(solution)/shard_map/analysis_inner/pallas_call | solution.py:102
  49.9 1.9 %collective-permute-start = (f32[80,8,128]{2,1,0:T(8,128)S(1)}, f32[80,8,128]{2,1,0:T(8,128)S(1)}, u32[]{:S(2)}, u32[]{:S(2)}) collective-permute-start(f32[80,8,128]{2,1,0:T(8,128)S(1)} %analysis_inner.1.inner_ref), channel_id=1, source_target_pairs={{0,1},{2,3},{4,5},{6,7},{8,9},{10,11},{12,13},{14,15},{16,17},{18,... | collective-permute-start | bytes 983048 | tf_op jit(solution)/shard_map/ppermute | solution.py:222
  51.9 1.6 %collective-permute-done.inside_ref = f32[80,8,128]{2,1,0:T(8,128)S(1)} collective-permute-done((f32[80,8,128]{2,1,0:T(8,128)S(1)}, f32[80,8,128]{2,1,0:T(8,128)S(1)}, u32[]{:S(2)}, u32[]{:S(2)}) %collective-permute-start) | collective-permute-done | bytes 327712 | tf_op jit(solution)/shard_map/ppermute | solution.py:222
  53.4 5.1 %collective-permute-done.1.outside_ref = f32[81,8,128]{2,1,0:T(8,128)S(1)} collective-permute-done((f32[81,8,128]{2,1,0:T(8,128)S(1)}, f32[81,8,128]{2,1,0:T(8,128)S(1)}, u32[]{:S(2)}, u32[]{:S(2)}) %collective-permute-start.1) | collective-permute-done | bytes 331808 | tf_op jit(solution)/shard_map/ppermute | solution.py:220
  58.6 0.0 copy-done
  58.6 2.9 %forecast.1 = f32[80,16,128]{2,1,0:T(8,128)} custom-call(s32[3]{0:T(128)S(1)} %add_convert_fusion.refs_0_.place_ref, f32[4,128]{1,0:T(4,128)S(1)} %copy-done, f32[80,8,128]{2,1,0:T(8,128)S(1)} %collective-permute-done.inside_ref, f32[81,8,128]{2,1,0:T(8,128)S(1)} %collective-permute-done.1.outside_ref, f32[80,8,128]{2,1,0:T(8,128)S(1)} %analysis_inner.1.inner_ref, ...), custom_call_target="tpu_custom_call" | custom-call | tf_op jit(solution)/shard_map/forecast/pallas_call | solution.py:193
Async XLA Ops:
  1.7 41.5 %copy-start.1 = (f32[2,16,32,16]{2,3,1,0:T(8,128)S(1)}, f32[2,16,32,16]{2,3,1,0:T(8,128)}, u32[]{:S(2)}) copy-start(f32[2,16,32,16]{2,3,1,0:T(8,128)} %param.8) | copy-start | bytes 196612
  43.2 0.7 %copy-start.2 = (s32[128]{0:T(128)S(1)}, s32[128]{0:T(128)}, u32[]{:S(2)}) copy-start(s32[128]{0:T(128)} %param.9) | copy-start | bytes 1540
  43.2 0.7 %copy-start.3 = (f32[128]{0:T(128)S(1)}, f32[128]{0:T(128)}, u32[]{:S(2)}) copy-start(f32[128]{0:T(128)} %param.10) | copy-start | bytes 1540
  45.9 12.7 %copy-start = (f32[4,128]{1,0:T(4,128)S(1)}, f32[4,128]{1,0:T(4,128)}, u32[]{:S(2)}) copy-start(f32[4,128]{1,0:T(4,128)} %viscosity_ref.1) | copy-start | bytes 6148
  45.9 12.7 %collective-permute-start.1 = (f32[81,8,128]{2,1,0:T(8,128)S(1)}, f32[81,8,128]{2,1,0:T(8,128)S(1)}, u32[]{:S(2)}, u32[]{:S(2)}) collective-permute-start(f32[81,8,128]{2,1,0:T(8,128)S(1)} %analysis_outer.1.outer_ref), channel_id=1, source_target_pairs={{1,2},{3,4},{5,6},{7,8},{9,10},{11,12},{13,14},{15,16},{17,18},{19... | collective-permute-start | bytes 995336 | tf_op jit(solution)/shard_map/ppermute | solution.py:220
  49.9 3.5 %collective-permute-start = (f32[80,8,128]{2,1,0:T(8,128)S(1)}, f32[80,8,128]{2,1,0:T(8,128)S(1)}, u32[]{:S(2)}, u32[]{:S(2)}) collective-permute-start(f32[80,8,128]{2,1,0:T(8,128)S(1)} %analysis_inner.1.inner_ref), channel_id=1, source_target_pairs={{0,1},{2,3},{4,5},{6,7},{8,9},{10,11},{12,13},{14,15},{16,17},{18,... | collective-permute-start | bytes 983048 | tf_op jit(solution)/shard_map/ppermute | solution.py:222

commit v4 on v3

--- a/solution.py
+++ b/solution.py
@@ -18,25 +18,34 @@
 SMEM = pl.BlockSpec(memory_space=pltpu.SMEM)
 
 
-def pick_kernel(ids_ref, states_ref, out_ref):
+def pick_kernel(ids_ref, states_ref, cell_ref, frac_ref, out_ref, table_ref):
+    odd = lax.axis_index("lat") % 2
+    make_table(odd, cell_ref, frac_ref, table_ref.at[0])
+    make_table(1 - odd, cell_ref, frac_ref, table_ref.at[1])
     for i in range(out_ref.shape[0]):
         out_ref[i] = states_ref[ids_ref[0, i]]
 
 
-def pick(states, src_ids):
+def pick(states, src_ids, cell, frac, points):
     return pl.pallas_call(
         pick_kernel,
-        out_shape=jax.ShapeDtypeStruct((src_ids.shape[1],) + states.shape[1:], states.dtype),
-        in_specs=[SMEM, VMEM],
-        out_specs=VMEM,
+        out_shape=(
+            jax.ShapeDtypeStruct((src_ids.shape[1],) + states.shape[1:], states.dtype),
+            jax.ShapeDtypeStruct((2, 6 * points, 2 * cell.shape[1]), jnp.float32),
+        ),
+        in_specs=[SMEM, VMEM, VMEM, VMEM],
+        out_specs=(VMEM, VMEM),
         name="pick",
-    )(src_ids, states)
-
-
-def make_weights(pair, coarse_ref, cell_ref, frac_ref, weights_ref):
-    members = weights_ref.shape[0]
-    nlon = cell_ref.shape[1]
-    points = coarse_ref.shape[0] // (2 * members)
+    )(src_ids, states, cell, frac)
+
+
+def halves(a):
+    big = a.astype(jnp.bfloat16).astype(jnp.float32)
+    return big, (a - big).astype(jnp.bfloat16).astype(jnp.float32)
+
+
+def make_table(pair, cell_ref, frac_ref, table_ref):
+    points, nlon = table_ref.shape[0] // 6, cell_ref.shape[1]
     point = lax.broadcasted_iota(jnp.int32, (points, nlon), 0)
     cell = jnp.broadcast_to(cell_ref[...], (points, nlon))
     frac = jnp.broadcast_to(frac_ref[...], (points, nlon))
@@ -47,23 +56,32 @@
         low.append((1.0 - t) * table)
         high.append(t * table)
     both = jnp.concatenate([jnp.concatenate(low, axis=1), jnp.concatenate(high, axis=1)], axis=0)
+    big, small = halves(both)
+    table_ref[:2 * points] = big
+    table_ref[2 * points:4 * points] = small
+    table_ref[4 * points:] = big
+
+
+def make_weights(coarse_ref, table_ref, weights_ref):
+    members = weights_ref.shape[0]
+    table = table_ref[...]
     for k in range(members):
-        rows = coarse_ref[pl.ds(k, 2 * points, stride=members), :]
-        product = lax.dot_general(
-            rows, both, (((0,), (0,)), ((), ())),
-            precision=lax.Precision.HIGHEST, preferred_element_type=jnp.float32)
+        big, small = halves(coarse_ref[pl.ds(k, table.shape[0] // 3, stride=members), :])
+        rows = jnp.concatenate([big, big, small], axis=0)
+        product = lax.dot_general(rows, table, (((0,), (0,)), ((), ())), preferred_element_type=jnp.float32)
         weights_ref[k] = product.reshape(weights_ref.shape[1:])
 
 
 def analysis_kernel(facing, block, *refs):
-    place_ref, coarse_ref, cell_ref, frac_ref, sources_ref, *out_refs = refs[:-2]
+    coarse_ref, table_ref, sources_ref, *out_refs = refs[:-2]
     weights_ref, wide_ref = refs[-2:]
-    pair = place_ref[2] if facing else 1 - place_ref[2]
+    odd = lax.axis_index("lat") % 2
+    pair = odd if facing else 1 - odd
     count = sources_ref.shape[0]
     sources = count // FIELDS
     members = weights_ref.shape[0]
     half, nlon = out_refs[0].shape[1:]
-    make_weights(pair, coarse_ref, cell_ref, frac_ref, weights_ref)
+    make_weights(coarse_ref, table_ref.at[0 if facing else 1], weights_ref)
     upper = lax.broadcasted_iota(jnp.int32, (half, nlon), 0) < LEV
     later = jnp.full((half, nlon), pair, jnp.int32) != 0
     for i in range(count):
@@ -95,15 +113,15 @@
         lax.fori_loop(0, share // block, functools.partial(some_members, start=i * share, out_ref=out_ref), 0)
 
 
-def analyse(facing, pieces, place, coarse, cell, frac, sources, members):
-    nlon = cell.shape[1]
+def analyse(facing, coarse, table, sources, members):
+    nlon = sources.shape[2]
     half = ROWS * LEV // 2
     count = sources.shape[0]
     return pl.pallas_call(
         functools.partial(analysis_kernel, facing, 4),
-        out_shape=[jax.ShapeDtypeStruct((members * FIELDS // pieces + (PAD if facing else 0), half, nlon), jnp.float32)] * pieces,
-        in_specs=[SMEM] + [VMEM] * 4,
-        out_specs=[VMEM] * pieces,
+        out_shape=jax.ShapeDtypeStruct((members * FIELDS + (PAD if facing else 0), half, nlon), jnp.float32),
+        in_specs=[VMEM] * 3,
+        out_specs=VMEM,
         scratch_shapes=[
             pltpu.VMEM((members, count // FIELDS // 8, 8, 2 * nlon), jnp.float32),
             pltpu.VMEM((count, half, nlon), jnp.float32),
@@ -111,19 +129,20 @@
         compiler_params=pltpu.CompilerParams(vmem_limit_bytes=VMEM_LIMIT),
         cost_estimate=pl.CostEstimate(flops=2 * 10**10, bytes_accessed=2 * 10**7, transcendentals=0),
         name="analysis_outer" if facing else "analysis_inner",
-    )(place, coarse, cell, frac, sources)
+    )(coarse, table, sources)
 
 
 def forecast_kernel(
-    group, place_ref, viscosity_ref, inside_ref, outside_ref, inner_ref, outer_ref, out_ref, result_ref, sem
+    group, viscosity_ref, inside_ref, outside_ref, inner_ref, outer_ref, out_ref, result_ref, sem
 ):
     count, half, nlon = inner_ref.shape
     members = count // FIELDS
     upper = lax.broadcasted_iota(jnp.int32, (half, nlon), 0) < LEV
     spread = 0.25 * jnp.concatenate([viscosity_ref[...]] * 2, axis=0)
     stay = 1.0 - 4.0 * spread
-    keep = jnp.where(upper, place_ref[1], place_ref[0]) != 0
-    odd = jnp.full((half, nlon), place_ref[2], jnp.int32) != 0
+    lat = lax.axis_index("lat")
+    keep = jnp.where(upper, lax.axis_size("lat") - 1 - lat, lat) != 0
+    odd = jnp.full((half, nlon), lat % 2, jnp.int32) != 0
 
     def swap(a):
         return pltpu.roll(a, LEV, 0)
@@ -188,39 +207,37 @@
         copy.wait()
 
 
-def forecast(place, viscosity, inside, outside, inner, outer, group=GROUP, parts=PARTS):
+def forecast(viscosity, inside, outside, inner, outer, group=GROUP, parts=PARTS):
     count, half, nlon = inner.shape
     return pl.pallas_call(
         functools.partial(forecast_kernel, group),
         out_shape=jax.ShapeDtypeStruct((count, 2 * half, nlon), jnp.float32),
-        in_specs=[SMEM] + [VMEM] * 5,
+        in_specs=[VMEM] * 5,
         out_specs=pl.BlockSpec(memory_space=pl.ANY),
         scratch_shapes=[pltpu.VMEM((count, 2 * half, nlon), jnp.float32), pltpu.SemaphoreType.DMA((parts,))],
         compiler_params=pltpu.CompilerParams(vmem_limit_bytes=VMEM_LIMIT),
         name="forecast",
-    )(place, viscosity, inside, outside, inner, outer)
+    )(viscosity, inside, outside, inner, outer)
 
 
 def on_device(states, src_ids, coarse_w, lon_cell, lon_frac, viscosity):
     members, fields, rows, lev, nlon = states.shape
     size = lax.axis_size("lat")
-    lat = lax.axis_index("lat")
-    place = jnp.stack([lat != 0, lat != size - 1, lat % 2 != 0]).astype(jnp.int32)
     coarse = jnp.swapaxes(coarse_w, 2, 3)
     coarse = coarse.reshape(-1, coarse.shape[3])
-    cell, frac = lon_cell[None], lon_frac[None]
-    picked = pick(states.reshape(members, fields, rows * lev, nlon), src_ids)
+    picked, table = pick(
+        states.reshape(members, fields, rows * lev, nlon), src_ids, lon_cell[None], lon_frac[None], coarse_w.shape[1])
     sources = lax.all_gather(picked, "mem")
     sources = sources.reshape(-1, rows * lev, nlon)
     across = [(i, i + 1) for i in range(1, size - 1, 2)]
     across += [(j, i) for i, j in across]
     within = [(i, i + 1) for i in range(0, size, 2)]
     within += [(j, i) for i, j in within]
-    outer, = analyse(True, 1, place, coarse, cell, frac, sources, members)
+    outer = analyse(True, coarse, table, sources, members)
     outside = lax.ppermute(outer, "lat", across)
-    inner, = analyse(False, 1, place, coarse, cell, frac, sources, members)
+    inner = analyse(False, coarse, table, sources, members)
     inside = lax.ppermute(inner, "lat", within)
-    out = forecast(place, viscosity, inside, outside, inner, outer)
+    out = forecast(viscosity, inside, outside, inner, outer)
     return out.reshape(members, fields, rows, lev, nlon)
 
 

time: 61.7 us -> 59.7 us (0.968)
  Pallas kernels: 8.67 us -> 6.47 us
  waiting for transfers between devices: 6.74 us -> 7.61 us
  local copies, waits for them, and re-layouts: 0.68 us -> 0.01 us
    pallas_call x3, Pallas kernels: 5.77 us -> 4.11 us  [the longest x2 2.36 us: analyse(): pl.pallas_call(functools.partial(analysis_kernel, facing, 4), out_shape=j...]
    ppermute x1, waiting for transfers between devices: 5.14 us -> 6.02 us  [on_device(): outside = lax.ppermute(outer, 'lat', across)]
    unnamed x8 -> x6, local copies, waits for them, and re-layouts: 0.68 us -> 0.01 us
  transfers between devices with their start and end apart: 2 -> 2, of which waited for: 2 -> 2; matrix products, arithmetic and copies ran while one was open for 0% -> 0% of each run, Pallas kernels for 3% -> 2%
where the time goes in v4:
time: 59.7 us; the launch traced here: 59.5 us
  blocking collectives  41.5 us (70%)
  waiting for transfers between devices  7.61 us (13%)
  Pallas kernels  6.47 us (11%)
  starting transfers between devices  3.84 us (6%)
    all_gather x1, blocking collectives, on_device(): sources = lax.all_gather(picked, 'mem')  41.5 us
    ppermute x1, waiting for transfers between devices, on_device(): outside = lax.ppermute(outer, 'lat', across)  6.02 us
    pallas_call x1, Pallas kernels, forecast(): pl.pallas_call(functools.partial(forecast_kernel, group), out_shape=jax.S...  2.37 us
    pallas_call x2, Pallas kernels, analyse(): pl.pallas_call(functools.partial(analysis_kernel, facing, 4), out_shape=j...  2.36 us
    ppermute x1, starting transfers between devices, on_device(): outside = lax.ppermute(outer, 'lat', across)  1.92 us
    ppermute x1, starting transfers between devices, on_device(): inside = lax.ppermute(inner, 'lat', within)  1.92 us
    pallas_call x1, Pallas kernels, pick(): pl.pallas_call(pick_kernel, out_shape=(jax.ShapeDtypeStruct((src_ids.shap...  1.75 us
    ppermute x1, waiting for transfers between devices, on_device(): inside = lax.ppermute(inner, 'lat', within)  1.59 us
  transfers between devices with their start and end apart: 2, of which 2 were waited for; matrix products, arithmetic and copies ran while one was open for 0% of the time, Pallas kernels for 2%

profile of v4, /device:TPU:64, one launch (start us, length us, event | category | flops | bytes accessed | tf_op | source)
XLA Modules:
  0.0 59.5 jit_solution(1488624999795812512)
XLA Ops:
  0.0 1.8 %pick.1 = (bf16[8,5,16,128]{3,2,1,0:T(8,128)(2,1)}, f32[2,96,256]{2,1,0:T(8,128)}) custom-call(s32[1,8]{1,0:T(1,128)} %ids_ref.1, bf16[16,5,16,128]{3,2,1,0:T(8,128)(2,1)} %bitcast.12, s32[1,128]{1,0:T(1,128)} %bitcast.13, f32[1,128]{1,0:T(1,128)} %bitcast.14), custom_call_target="tpu_custom_call" | custom-call | tf_op jit(solution)/shard_map/pick/pallas_call | solution.py:30
  1.8 0.0 copy-start.1
  1.8 0.0 copy-start.2
  1.8 41.5 %all-gather = bf16[32,5,16,128]{3,2,1,0:T(8,128)(2,1)S(1)} all-gather(bf16[8,5,16,128]{3,2,1,0:T(8,128)(2,1)} %get-tuple-element.8), channel_id=2, replica_groups=mesh['mem'=4,'lat'=256] {'mem'}, dimensions={0}, use_global_device_ids=true | all-gather | bytes 819200 | tf_op jit(solution)/shard_map/all_gather | solution.py:230
  43.3 0.0 copy-done.1
  43.3 0.0 copy-done.2
  43.3 1.2 %analysis_outer.1.outer_ref = f32[81,8,128]{2,1,0:T(8,128)S(1)} custom-call(f32[512,32]{1,0:T(8,128)S(1)} %bitcast.10, f32[2,96,256]{2,1,0:T(8,128)S(1)} %copy-done.2, bf16[160,16,128]{2,1,0:T(8,128)(2,1)S(1)} %bitcast.8), custom_call_target="tpu_custom_call" | custom-call | flops 20000000000 | bytes 20000000 | tf_op jit(solution)/shard_map/analysis_outer/pallas_call | solution.py:120
  44.5 0.0 copy-start
  44.5 1.9 %collective-permute-start.1 = (f32[81,8,128]{2,1,0:T(8,128)S(1)}, f32[81,8,128]{2,1,0:T(8,128)S(1)}, u32[]{:S(2)}, u32[]{:S(2)}) collective-permute-start(f32[81,8,128]{2,1,0:T(8,128)S(1)} %analysis_outer.1.outer_ref), channel_id=1, source_target_pairs={{1,2},{3,4},{5,6},{7,8},{9,10},{11,12},{13,14},{15,16},{17,18},{19... | collective-permute-start | bytes 995336 | tf_op jit(solution)/shard_map/ppermute | solution.py:237
  46.4 1.2 %analysis_inner.1.inner_ref = f32[80,8,128]{2,1,0:T(8,128)S(1)} custom-call(f32[512,32]{1,0:T(8,128)S(1)} %bitcast.11, f32[2,96,256]{2,1,0:T(8,128)S(1)} %copy-done.2, bf16[160,16,128]{2,1,0:T(8,128)(2,1)S(1)} %bitcast.9), custom_call_target="tpu_custom_call" | custom-call | flops 20000000000 | bytes 20000000 | tf_op jit(solution)/shard_map/analysis_inner/pallas_call | solution.py:120
  47.6 1.9 %collective-permute-start = (f32[80,8,128]{2,1,0:T(8,128)S(1)}, f32[80,8,128]{2,1,0:T(8,128)S(1)}, u32[]{:S(2)}, u32[]{:S(2)}) collective-permute-start(f32[80,8,128]{2,1,0:T(8,128)S(1)} %analysis_inner.1.inner_ref), channel_id=1, source_target_pairs={{0,1},{2,3},{4,5},{6,7},{8,9},{10,11},{12,13},{14,15},{16,17},{18,... | collective-permute-start | bytes 983048 | tf_op jit(solution)/shard_map/ppermute | solution.py:239
  49.5 1.6 %collective-permute-done.inside_ref = f32[80,8,128]{2,1,0:T(8,128)S(1)} collective-permute-done((f32[80,8,128]{2,1,0:T(8,128)S(1)}, f32[80,8,128]{2,1,0:T(8,128)S(1)}, u32[]{:S(2)}, u32[]{:S(2)}) %collective-permute-start) | collective-permute-done | bytes 327712 | tf_op jit(solution)/shard_map/ppermute | solution.py:239
  51.1 6.0 %collective-permute-done.1.outside_ref = f32[81,8,128]{2,1,0:T(8,128)S(1)} collective-permute-done((f32[81,8,128]{2,1,0:T(8,128)S(1)}, f32[81,8,128]{2,1,0:T(8,128)S(1)}, u32[]{:S(2)}, u32[]{:S(2)}) %collective-permute-start.1) | collective-permute-done | bytes 331808 | tf_op jit(solution)/shard_map/ppermute | solution.py:237
  57.2 0.0 copy-done
  57.2 2.4 %forecast.1 = f32[80,16,128]{2,1,0:T(8,128)} custom-call(f32[4,128]{1,0:T(4,128)S(1)} %copy-done, f32[80,8,128]{2,1,0:T(8,128)S(1)} %collective-permute-done.inside_ref, f32[81,8,128]{2,1,0:T(8,128)S(1)} %collective-permute-done.1.outside_ref, f32[80,8,128]{2,1,0:T(8,128)S(1)} %analysis_inner.1.inner_ref, f32[81,8,128]{2,1,0:T(8,128)S(1)} %analysis_outer.1.outer_ref), custom_call_target="tpu_custom_call" | custom-call | tf_op jit(solution)/shard_map/forecast/pallas_call | solution.py:212
Async XLA Ops:
  1.8 41.5 %copy-start.1 = (f32[2,16,32,16]{2,3,1,0:T(8,128)S(1)}, f32[2,16,32,16]{2,3,1,0:T(8,128)}, u32[]{:S(2)}) copy-start(f32[2,16,32,16]{2,3,1,0:T(8,128)} %param.8) | copy-start | bytes 196612
  1.8 41.5 %copy-start.2 = (f32[2,96,256]{2,1,0:T(8,128)S(1)}, f32[2,96,256]{2,1,0:T(8,128)}, u32[]{:S(2)}) copy-start(f32[2,96,256]{2,1,0:T(8,128)} %get-tuple-element.7.refs_1_) | copy-start | bytes 589828
  44.5 12.7 %copy-start = (f32[4,128]{1,0:T(4,128)S(1)}, f32[4,128]{1,0:T(4,128)}, u32[]{:S(2)}) copy-start(f32[4,128]{1,0:T(4,128)} %viscosity_ref.1) | copy-start | bytes 6148
  44.5 12.7 %collective-permute-start.1 = (f32[81,8,128]{2,1,0:T(8,128)S(1)}, f32[81,8,128]{2,1,0:T(8,128)S(1)}, u32[]{:S(2)}, u32[]{:S(2)}) collective-permute-start(f32[81,8,128]{2,1,0:T(8,128)S(1)} %analysis_outer.1.outer_ref), channel_id=1, source_target_pairs={{1,2},{3,4},{5,6},{7,8},{9,10},{11,12},{13,14},{15,16},{17,18},{19... | collective-permute-start | bytes 995336 | tf_op jit(solution)/shard_map/ppermute | solution.py:237
  47.6 3.5 %collective-permute-start = (f32[80,8,128]{2,1,0:T(8,128)S(1)}, f32[80,8,128]{2,1,0:T(8,128)S(1)}, u32[]{:S(2)}, u32[]{:S(2)}) collective-permute-start(f32[80,8,128]{2,1,0:T(8,128)S(1)} %analysis_inner.1.inner_ref), channel_id=1, source_target_pairs={{0,1},{2,3},{4,5},{6,7},{8,9},{10,11},{12,13},{14,15},{16,17},{18,... | collective-permute-start | bytes 983048 | tf_op jit(solution)/shard_map/ppermute | solution.py:239

commit v5 on v4

--- a/solution.py
+++ b/solution.py
@@ -132,60 +132,115 @@
     )(coarse, table, sources)
 
 
-def forecast_kernel(
-    group, viscosity_ref, inside_ref, outside_ref, inner_ref, outer_ref, out_ref, result_ref, sem
-):
-    count, half, nlon = inner_ref.shape
-    members = count // FIELDS
+def constants(viscosity_ref, half, nlon):
     upper = lax.broadcasted_iota(jnp.int32, (half, nlon), 0) < LEV
     spread = 0.25 * jnp.concatenate([viscosity_ref[...]] * 2, axis=0)
+    odd = jnp.full((half, nlon), lax.axis_index("lat") % 2, jnp.int32) != 0
+    return upper, spread, odd
+
+
+def swap(a):
+    return pltpu.roll(a, LEV, 0)
+
+
+def choose(mask, a, b):
+    return [jnp.where(mask, x, y) for x, y in zip(a, b)]
+
+
+def advance(spread, centre, north, south):
     stay = 1.0 - 4.0 * spread
+    west = [pltpu.roll(a, 1, 1) for a in centre]
+    east = [pltpu.roll(a, a.shape[1] - 1, 1) for a in centre]
+    dx = [e - w for e, w in zip(east, west)]
+    dy = [n - s for n, s in zip(north, south)]
+    u, v = centre[0] * -0.125, centre[1] * -0.125
+    out = []
+    for f in range(FIELDS):
+        around = (east[f] + west[f]) + (north[f] + south[f])
+        out.append(stay * centre[f] + spread * around + (u * dx[f] + v * dy[f]))
+    out[0] = out[0] - 0.125 * dx[2]
+    out[1] = out[1] - 0.125 * dy[2]
+    out[2] = out[2] - 0.125 * (dx[0] + dy[1])
+    return out
+
+
+def begin_kernel(group, viscosity_ref, inside_ref, inner_ref, outer_ref, first_ref, last_ref, near_ref):
+    count, half, nlon = inner_ref.shape
+    upper, spread, odd = constants(viscosity_ref, half, nlon)
+    fields = range(FIELDS)
+
+    def one_member(k):
+        base = k * FIELDS
+        outer = [outer_ref[base + f] for f in fields]
+        inner = [inner_ref[base + f] for f in fields]
+        inside = [swap(inside_ref[base + f]) for f in fields]
+        first, last = choose(odd, inner, outer), choose(odd, outer, inner)
+        before = [jnp.where(odd, a, 0.0) for a in inside]
+        after = [jnp.where(odd, 0.0, a) for a in inside]
+        sf, sl = [swap(a) for a in first], [swap(a) for a in last]
+        middle = choose(upper, sf, sl)
+        first1 = advance(spread, first, middle, choose(upper, before, sf))
+        last1 = advance(spread, last, choose(upper, sl, after), middle)
+        near = choose(upper, sl, sf)
+        for f in fields:
+            first_ref[base + f] = first1[f]
+            last_ref[base + f] = last1[f]
+            near_ref[base + f] = near[f]
+
+    def some(i, carry):
+        for j in range(group):
+            one_member(i * group + j)
+        return carry
+
+    lax.fori_loop(0, count // FIELDS // group, some, 0)
+
+
+def begin(viscosity, inside, inner, outer):
+    return pl.pallas_call(
+        functools.partial(begin_kernel, GROUP),
+        out_shape=[jax.ShapeDtypeStruct(inner.shape, jnp.float32)] * 3,
+        in_specs=[VMEM] * 4,
+        out_specs=[VMEM] * 3,
+        compiler_params=pltpu.CompilerParams(vmem_limit_bytes=VMEM_LIMIT),
+        cost_estimate=pl.CostEstimate(flops=1, bytes_accessed=1, transcendentals=0),
+        name="begin",
+    )(viscosity, inside, inner, outer)
+
+
+def finish_kernel(
+    group, viscosity_ref, outside_ref, inside_ref, outer_ref, first_ref, last_ref, near_ref, out_ref, result_ref, sem
+):
+    count, half, nlon = near_ref.shape
+    members = count // FIELDS
+    upper, spread, odd = constants(viscosity_ref, half, nlon)
     lat = lax.axis_index("lat")
     keep = jnp.where(upper, lax.axis_size("lat") - 1 - lat, lat) != 0
-    odd = jnp.full((half, nlon), lat % 2, jnp.int32) != 0
-
-    def swap(a):
-        return pltpu.roll(a, LEV, 0)
-
-    def advance(centre, north, south):
-        west = [pltpu.roll(a, 1, 1) for a in centre]
-        east = [pltpu.roll(a, nlon - 1, 1) for a in centre]
-        dx = [e - w for e, w in zip(east, west)]
-        dy = [n - s for n, s in zip(north, south)]
-        u, v = centre[0] * -0.125, centre[1] * -0.125
-        out = []
-        for f in range(FIELDS):
-            around = (east[f] + west[f]) + (north[f] + south[f])
-            out.append(stay * centre[f] + spread * around + (u * dx[f] + v * dy[f]))
-        out[0] = out[0] - 0.125 * dx[2]
-        out[1] = out[1] - 0.125 * dy[2]
-        out[2] = out[2] - 0.125 * (dx[0] + dy[1])
-        return out
-
-    def mix(a, b):
-        return [jnp.where(upper, x, y) for x, y in zip(a, b)]
+    here = upper != odd
+    sign = jnp.where(odd, 0.125, -0.125)
+    fields = range(FIELDS)
 
     def one_member(k):
         base = k * FIELDS
-        fields = range(FIELDS)
-        outer = [outer_ref[base + f] for f in fields]
-        inner = [inner_ref[base + f] for f in fields]
         outside = [outside_ref[base + f] for f in fields]
         inside = [inside_ref[base + f] for f in fields]
-        first = [jnp.where(odd, inner[f], outer[f]) for f in fields]
-        last = [jnp.where(odd, outer[f], inner[f]) for f in fields]
-        before = [jnp.where(odd, inside[f], outside[f]) for f in fields]
-        after = [jnp.where(odd, outside[f], inside[f]) for f in fields]
-        edge = mix(after, before)
-        sf, sl = [swap(a) for a in first], [swap(a) for a in last]
-        sb, sa = [swap(a) for a in before], [swap(a) for a in after]
-        first1 = advance(first, mix(sf, sl), mix(sb, sf))
-        last1 = advance(last, mix(sl, sa), mix(sf, sl))
-        edge1 = advance(edge, mix(sa, sf), mix(sl, sb))
+        first1 = [first_ref[base + f] for f in fields]
+        last1 = [last_ref[base + f] for f in fields]
+        near = [near_ref[base + f] for f in fields]
+        edge = choose(here, inside, outside)
+        beyond = [swap(a) for a in choose(here, outside, inside)]
+        added = [jnp.where(here, swap(a), 0.0) for a in edge]
+        weight = spread - sign * outer_ref[base + 1]
+        more = [weight * a for a in added]
+        more[1] = more[1] - sign * added[2]
+        more[2] = more[2] - sign * added[1]
+        first1 = [jnp.where(odd, a, a + m) for a, m in zip(first1, more)]
+        last1 = [jnp.where(odd, a + m, a) for a, m in zip(last1, more)]
+        edge1 = advance(spread, edge, choose(upper, beyond, near), choose(upper, near, beyond))
         edge1 = [jnp.where(keep, a, 0.0) for a in edge1]
         sf, sl, se = [swap(a) for a in first1], [swap(a) for a in last1], [swap(a) for a in edge1]
-        first2 = advance(first1, mix(sf, sl), mix(se, sf))
-        last2 = advance(last1, mix(sl, se), mix(sf, sl))
+        middle = choose(upper, sf, sl)
+        first2 = advance(spread, first1, middle, choose(upper, se, sf))
+        last2 = advance(spread, last1, choose(upper, sl, se), middle)
         for f in fields:
             result_ref[base + f, :half, :] = first2[f]
             result_ref[base + f, half:, :] = last2[f]
@@ -207,17 +262,17 @@
         copy.wait()
 
 
-def forecast(viscosity, inside, outside, inner, outer, group=GROUP, parts=PARTS):
-    count, half, nlon = inner.shape
+def finish(viscosity, outside, inside, outer, first, last, near):
+    count, half, nlon = near.shape
     return pl.pallas_call(
-        functools.partial(forecast_kernel, group),
+        functools.partial(finish_kernel, GROUP),
         out_shape=jax.ShapeDtypeStruct((count, 2 * half, nlon), jnp.float32),
-        in_specs=[VMEM] * 5,
+        in_specs=[VMEM] * 7,
         out_specs=pl.BlockSpec(memory_space=pl.ANY),
-        scratch_shapes=[pltpu.VMEM((count, 2 * half, nlon), jnp.float32), pltpu.SemaphoreType.DMA((parts,))],
+        scratch_shapes=[pltpu.VMEM((count, 2 * half, nlon), jnp.float32), pltpu.SemaphoreType.DMA((PARTS,))],
         compiler_params=pltpu.CompilerParams(vmem_limit_bytes=VMEM_LIMIT),
-        name="forecast",
-    )(viscosity, inside, outside, inner, outer)
+        name="finish",
+    )(viscosity, outside, inside, outer, first, last, near)
 
 
 def on_device(states, src_ids, coarse_w, lon_cell, lon_frac, viscosity):
@@ -237,7 +292,8 @@
     outside = lax.ppermute(outer, "lat", across)
     inner = analyse(False, coarse, table, sources, members)
     inside = lax.ppermute(inner, "lat", within)
-    out = forecast(viscosity, inside, outside, inner, outer)
+    first, last, near = begin(viscosity, inside, inner, outer)
+    out = finish(viscosity, outside, inside, outer, first, last, near)
     return out.reshape(members, fields, rows, lev, nlon)
 
 

time: 59.7 us -> 59.2 us (level)
  waiting for transfers between devices: 7.61 us -> 6.67 us
    ppermute x1, waiting for transfers between devices: 6.02 us -> 5.07 us  [on_device(): outside = lax.ppermute(outer, 'lat', across)]
    pallas_call x1 -> x2, Pallas kernels: 2.37 us -> 2.83 us  [the longest x1 1.9 us: finish(): pl.pallas_call(functools.partial(finish_kernel, GROUP), out_shape=jax.Sha...]
  transfers between devices with their start and end apart: 2 -> 2, of which waited for: 2 -> 2; matrix products, arithmetic and copies ran while one was open for 0% -> 0% of each run, Pallas kernels for 2% -> 4%
where the time goes in v5:
time: 59.2 us; the launch traced here: 59.1 us
  blocking collectives  41.5 us (70%)
  Pallas kernels  6.94 us (12%)
  waiting for transfers between devices  6.67 us (11%)
  starting transfers between devices  3.84 us (6%)
    all_gather x1, blocking collectives, on_device(): sources = lax.all_gather(picked, 'mem')  41.5 us
    ppermute x1, waiting for transfers between devices, on_device(): outside = lax.ppermute(outer, 'lat', across)  5.07 us
    pallas_call x2, Pallas kernels, analyse(): pl.pallas_call(functools.partial(analysis_kernel, facing, 4), out_shape=j...  2.36 us
    ppermute x1, starting transfers between devices, on_device(): outside = lax.ppermute(outer, 'lat', across)  1.92 us
    ppermute x1, starting transfers between devices, on_device(): inside = lax.ppermute(inner, 'lat', within)  1.92 us
    pallas_call x1, Pallas kernels, finish(): pl.pallas_call(functools.partial(finish_kernel, GROUP), out_shape=jax.Sha...  1.9 us
    pallas_call x1, Pallas kernels, pick(): pl.pallas_call(pick_kernel, out_shape=(jax.ShapeDtypeStruct((src_ids.shap...  1.75 us
    ppermute x1, waiting for transfers between devices, on_device(): inside = lax.ppermute(inner, 'lat', within)  1.59 us
  transfers between devices with their start and end apart: 2, of which 2 were waited for; matrix products, arithmetic and copies ran while one was open for 0% of the time, Pallas kernels for 4%

profile of v5, /device:TPU:64, one launch (start us, length us, event | category | flops | bytes accessed | tf_op | source)
XLA Modules:
  0.0 59.1 jit_solution(9405191311888973131)
XLA Ops:
  0.0 1.8 %pick.1 = (bf16[8,5,16,128]{3,2,1,0:T(8,128)(2,1)}, f32[2,96,256]{2,1,0:T(8,128)}) custom-call(s32[1,8]{1,0:T(1,128)} %ids_ref.1, bf16[16,5,16,128]{3,2,1,0:T(8,128)(2,1)} %bitcast.12, s32[1,128]{1,0:T(1,128)} %bitcast.13, f32[1,128]{1,0:T(1,128)} %bitcast.14), custom_call_target="tpu_custom_call" | custom-call | tf_op jit(solution)/shard_map/pick/pallas_call | solution.py:30
  1.8 0.0 copy-start.1
  1.8 0.0 copy-start.2
  1.8 41.5 %all-gather = bf16[32,5,16,128]{3,2,1,0:T(8,128)(2,1)S(1)} all-gather(bf16[8,5,16,128]{3,2,1,0:T(8,128)(2,1)} %get-tuple-element.11), channel_id=2, replica_groups=mesh['mem'=4,'lat'=256] {'mem'}, dimensions={0}, use_global_device_ids=true | all-gather | bytes 819200 | tf_op jit(solution)/shard_map/all_gather | solution.py:285
  43.3 0.0 copy-done.1
  43.3 0.0 copy-done.2
  43.3 1.2 %analysis_outer.1.outer_ref = f32[81,8,128]{2,1,0:T(8,128)S(1)} custom-call(f32[512,32]{1,0:T(8,128)S(1)} %bitcast.10, f32[2,96,256]{2,1,0:T(8,128)S(1)} %copy-done.2, bf16[160,16,128]{2,1,0:T(8,128)(2,1)S(1)} %bitcast.8), custom_call_target="tpu_custom_call" | custom-call | flops 20000000000 | bytes 20000000 | tf_op jit(solution)/shard_map/analysis_outer/pallas_call | solution.py:120
  44.5 0.0 copy-start
  44.5 1.9 %collective-permute-start = (f32[81,8,128]{2,1,0:T(8,128)S(1)}, f32[81,8,128]{2,1,0:T(8,128)S(1)}, u32[]{:S(2)}, u32[]{:S(2)}) collective-permute-start(f32[81,8,128]{2,1,0:T(8,128)S(1)} %analysis_outer.1.outer_ref), channel_id=1, source_target_pairs={{1,2},{3,4},{5,6},{7,8},{9,10},{11,12},{13,14},{15,16},{17,18},{19... | collective-permute-start | bytes 995336 | tf_op jit(solution)/shard_map/ppermute | solution.py:292
  46.4 1.2 %analysis_inner.1.inner_ref = f32[80,8,128]{2,1,0:T(8,128)S(1)} custom-call(f32[512,32]{1,0:T(8,128)S(1)} %bitcast.11, f32[2,96,256]{2,1,0:T(8,128)S(1)} %copy-done.2, bf16[160,16,128]{2,1,0:T(8,128)(2,1)S(1)} %bitcast.9), custom_call_target="tpu_custom_call" | custom-call | flops 20000000000 | bytes 20000000 | tf_op jit(solution)/shard_map/analysis_inner/pallas_call | solution.py:120
  47.6 1.9 %collective-permute-start.1 = (f32[80,8,128]{2,1,0:T(8,128)S(1)}, f32[80,8,128]{2,1,0:T(8,128)S(1)}, u32[]{:S(2)}, u32[]{:S(2)}) collective-permute-start(f32[80,8,128]{2,1,0:T(8,128)S(1)} %analysis_inner.1.inner_ref), channel_id=1, source_target_pairs={{0,1},{2,3},{4,5},{6,7},{8,9},{10,11},{12,13},{14,15},{16,17},{18,... | collective-permute-start | bytes 983048 | tf_op jit(solution)/shard_map/ppermute | solution.py:294
  49.5 1.6 %collective-permute-done.1.inside_ref = f32[80,8,128]{2,1,0:T(8,128)S(1)} collective-permute-done((f32[80,8,128]{2,1,0:T(8,128)S(1)}, f32[80,8,128]{2,1,0:T(8,128)S(1)}, u32[]{:S(2)}, u32[]{:S(2)}) %collective-permute-start.1) | collective-permute-done | bytes 327712 | tf_op jit(solution)/shard_map/ppermute | solution.py:294
  51.1 0.0 copy-done
  51.1 0.9 %begin.1 = (f32[80,8,128]{2,1,0:T(8,128)S(1)}, f32[80,8,128]{2,1,0:T(8,128)S(1)}, f32[80,8,128]{2,1,0:T(8,128)S(1)}) custom-call(f32[4,128]{1,0:T(4,128)S(1)} %copy-done, f32[80,8,128]{2,1,0:T(8,128)S(1)} %collective-permute-done.1.inside_ref, f32[80,8,128]{2,1,0:T(8,128)S(1)} %analysis_inner.1.inner_ref, f32[81,8,128]{2,1,0:T(8,128)S(1)} %analysis_outer.1.outer_ref), custom_call_target="tpu_custom_call" | custom-call | flops 1 | bytes 1 | tf_op jit(solution)/shard_map/begin/pallas_call | solution.py:199
  52.1 5.1 %collective-permute-done.outside_ref = f32[81,8,128]{2,1,0:T(8,128)S(1)} collective-permute-done((f32[81,8,128]{2,1,0:T(8,128)S(1)}, f32[81,8,128]{2,1,0:T(8,128)S(1)}, u32[]{:S(2)}, u32[]{:S(2)}) %collective-permute-start) | collective-permute-done | bytes 331808 | tf_op jit(solution)/shard_map/ppermute | solution.py:292
  57.2 1.9 %finish.1 = f32[80,16,128]{2,1,0:T(8,128)} custom-call(f32[4,128]{1,0:T(4,128)S(1)} %copy-done, f32[81,8,128]{2,1,0:T(8,128)S(1)} %collective-permute-done.outside_ref, f32[80,8,128]{2,1,0:T(8,128)S(1)} %collective-permute-done.1.inside_ref, f32[81,8,128]{2,1,0:T(8,128)S(1)} %analysis_outer.1.outer_ref, f32[80,8,128]{2,1,0:T(8,128)S(1)} %get-tuple-element.12.first_ref, ...), custom_call_target="tpu_custom_call" | custom-call | tf_op jit(solution)/shard_map/finish/pallas_call | solution.py:267
Async XLA Ops:
  1.8 41.5 %copy-start.1 = (f32[2,16,32,16]{2,3,1,0:T(8,128)S(1)}, f32[2,16,32,16]{2,3,1,0:T(8,128)}, u32[]{:S(2)}) copy-start(f32[2,16,32,16]{2,3,1,0:T(8,128)} %param.8) | copy-start | bytes 196612
  1.8 41.5 %copy-start.2 = (f32[2,96,256]{2,1,0:T(8,128)S(1)}, f32[2,96,256]{2,1,0:T(8,128)}, u32[]{:S(2)}) copy-start(f32[2,96,256]{2,1,0:T(8,128)} %get-tuple-element.10.refs_1_) | copy-start | bytes 589828
  44.5 6.7 %copy-start = (f32[4,128]{1,0:T(4,128)S(1)}, f32[4,128]{1,0:T(4,128)}, u32[]{:S(2)}) copy-start(f32[4,128]{1,0:T(4,128)} %viscosity_ref.3) | copy-start | bytes 6148
  44.5 12.7 %collective-permute-start = (f32[81,8,128]{2,1,0:T(8,128)S(1)}, f32[81,8,128]{2,1,0:T(8,128)S(1)}, u32[]{:S(2)}, u32[]{:S(2)}) collective-permute-start(f32[81,8,128]{2,1,0:T(8,128)S(1)} %analysis_outer.1.outer_ref), channel_id=1, source_target_pairs={{1,2},{3,4},{5,6},{7,8},{9,10},{11,12},{13,14},{15,16},{17,18},{19... | collective-permute-start | bytes 995336 | tf_op jit(solution)/shard_map/ppermute | solution.py:292
  47.6 3.5 %collective-permute-start.1 = (f32[80,8,128]{2,1,0:T(8,128)S(1)}, f32[80,8,128]{2,1,0:T(8,128)S(1)}, u32[]{:S(2)}, u32[]{:S(2)}) collective-permute-start(f32[80,8,128]{2,1,0:T(8,128)S(1)} %analysis_inner.1.inner_ref), channel_id=1, source_target_pairs={{0,1},{2,3},{4,5},{6,7},{8,9},{10,11},{12,13},{14,15},{16,17},{18,... | collective-permute-start | bytes 983048 | tf_op jit(solution)/shard_map/ppermute | solution.py:294

commit v6 on v5

--- a/solution.py
+++ b/solution.py
@@ -73,28 +73,27 @@
 
 
 def analysis_kernel(facing, block, *refs):
-    coarse_ref, table_ref, sources_ref, *out_refs = refs[:-2]
-    weights_ref, wide_ref = refs[-2:]
+    coarse_ref, table_ref, sources_ref, out_ref, send_ref, weights_ref, wide_ref = refs
     odd = lax.axis_index("lat") % 2
     pair = odd if facing else 1 - odd
     count = sources_ref.shape[0]
     sources = count // FIELDS
     members = weights_ref.shape[0]
-    half, nlon = out_refs[0].shape[1:]
+    half, nlon = out_ref.shape[1:]
     make_weights(coarse_ref, table_ref.at[0 if facing else 1], weights_ref)
     upper = lax.broadcasted_iota(jnp.int32, (half, nlon), 0) < LEV
     later = jnp.full((half, nlon), pair, jnp.int32) != 0
     for i in range(count):
         whole = sources_ref[i].astype(jnp.float32)
         wide_ref[i] = jnp.where(later, whole[half:], whole[:half])
-    share = members // len(out_refs)
-
-    def some_members(b, carry, start, out_ref):
+    near = upper != later
+
+    def some_members(b, carry):
         totals = [[None] * FIELDS for _ in range(block)]
         for s in range(sources):
             fields = [wide_ref[s * FIELDS + f] for f in range(FIELDS)]
             for j in range(block):
-                row = weights_ref.at[start + b * block + j, s // 8]
+                row = weights_ref.at[b * block + j, s // 8]
                 low, high = [
                     jnp.broadcast_to(row[s % 8:s % 8 + 1, i * nlon:(i + 1) * nlon], (half, nlon)) for i in range(2)
                 ]
@@ -102,15 +101,35 @@
                 for f in range(FIELDS):
                     term = w * fields[f]
                     totals[j][f] = term if s == 0 else totals[j][f] + term
-        for j in range(block):
-            for f in range(FIELDS):
-                out_ref[(b * block + j) * FIELDS + f] = totals[j][f]
+        items = [totals[j][f] for j in range(block) for f in range(FIELDS)]
+        for i, item in enumerate(items):
+            out_ref[b * len(items) + i] = item
+        for i in range(0, len(items), 4):
+            tile = (b * len(items) + i) // 4 * 3
+            four = items[i:i + 4]
+            rest = [a - a.astype(jnp.bfloat16).astype(jnp.float32) for a in four]
+            rest = [jnp.where(near, rest[j], swap(rest[j + 1])) for j in (0, 2)]
+            for j, two in enumerate((four[:2], four[2:], rest)):
+                send_ref[tile + j] = jnp.concatenate(two, axis=0).astype(jnp.bfloat16)
         return carry
 
     if facing:
-        out_refs[0][members * FIELDS:] = jnp.zeros((PAD, half, nlon), jnp.float32)
-    for i, out_ref in enumerate(out_refs):
-        lax.fori_loop(0, share // block, functools.partial(some_members, start=i * share, out_ref=out_ref), 0)
+        send_ref[send_ref.shape[0] - PAD:] = jnp.zeros((PAD, 2 * half, nlon), jnp.bfloat16)
+    lax.fori_loop(0, members // block, some_members, 0)
+
+
+def receive(near, send_ref, out_ref):
+    half = out_ref.shape[1]
+
+    def four(g, carry):
+        tiles = [send_ref[3 * g + j].astype(jnp.float32) for j in range(3)]
+        for i in range(4):
+            rest = tiles[2][i // 2 * half:(i // 2 + 1) * half]
+            rest = jnp.where(near, swap(rest) if i % 2 else rest, 0.0)
+            out_ref[4 * g + i] = tiles[i // 2][i % 2 * half:(i % 2 + 1) * half] + rest
+        return carry
+
+    lax.fori_loop(0, out_ref.shape[0] // 4, four, 0, unroll=5)
 
 
 def analyse(facing, coarse, table, sources, members):
@@ -119,9 +138,12 @@
     count = sources.shape[0]
     return pl.pallas_call(
         functools.partial(analysis_kernel, facing, 4),
-        out_shape=jax.ShapeDtypeStruct((members * FIELDS + (PAD if facing else 0), half, nlon), jnp.float32),
+        out_shape=(
+            jax.ShapeDtypeStruct((members * FIELDS, half, nlon), jnp.float32),
+            jax.ShapeDtypeStruct((members * FIELDS // 4 * 3 + (PAD if facing else 0), 2 * half, nlon), jnp.bfloat16),
+        ),
         in_specs=[VMEM] * 3,
-        out_specs=VMEM,
+        out_specs=(VMEM, VMEM),
         scratch_shapes=[
             pltpu.VMEM((members, count // FIELDS // 8, 8, 2 * nlon), jnp.float32),
             pltpu.VMEM((count, half, nlon), jnp.float32),
@@ -164,9 +186,10 @@
     return out
 
 
-def begin_kernel(group, viscosity_ref, inside_ref, inner_ref, outer_ref, first_ref, last_ref, near_ref):
+def begin_kernel(group, viscosity_ref, sent_ref, inner_ref, outer_ref, first_ref, last_ref, near_ref, inside_ref):
     count, half, nlon = inner_ref.shape
     upper, spread, odd = constants(viscosity_ref, half, nlon)
+    receive(upper != odd, sent_ref, inside_ref)
     fields = range(FIELDS)
 
     def one_member(k):
@@ -198,9 +221,9 @@
 def begin(viscosity, inside, inner, outer):
     return pl.pallas_call(
         functools.partial(begin_kernel, GROUP),
-        out_shape=[jax.ShapeDtypeStruct(inner.shape, jnp.float32)] * 3,
+        out_shape=[jax.ShapeDtypeStruct(inner.shape, jnp.float32)] * 4,
         in_specs=[VMEM] * 4,
-        out_specs=[VMEM] * 3,
+        out_specs=[VMEM] * 4,
         compiler_params=pltpu.CompilerParams(vmem_limit_bytes=VMEM_LIMIT),
         cost_estimate=pl.CostEstimate(flops=1, bytes_accessed=1, transcendentals=0),
         name="begin",
@@ -208,7 +231,8 @@
 
 
 def finish_kernel(
-    group, viscosity_ref, outside_ref, inside_ref, outer_ref, first_ref, last_ref, near_ref, out_ref, result_ref, sem
+    group, viscosity_ref, sent_ref, inside_ref, outer_ref, first_ref, last_ref, near_ref,
+    out_ref, outside_ref, result_ref, sem
 ):
     count, half, nlon = near_ref.shape
     members = count // FIELDS
@@ -216,6 +240,7 @@
     lat = lax.axis_index("lat")
     keep = jnp.where(upper, lax.axis_size("lat") - 1 - lat, lat) != 0
     here = upper != odd
+    receive(upper == odd, sent_ref, outside_ref)
     sign = jnp.where(odd, 0.125, -0.125)
     fields = range(FIELDS)
 
@@ -269,7 +294,11 @@
         out_shape=jax.ShapeDtypeStruct((count, 2 * half, nlon), jnp.float32),
         in_specs=[VMEM] * 7,
         out_specs=pl.BlockSpec(memory_space=pl.ANY),
-        scratch_shapes=[pltpu.VMEM((count, 2 * half, nlon), jnp.float32), pltpu.SemaphoreType.DMA((PARTS,))],
+        scratch_shapes=[
+            pltpu.VMEM((count, half, nlon), jnp.float32),
+            pltpu.VMEM((count, 2 * half, nlon), jnp.float32),
+            pltpu.SemaphoreType.DMA((PARTS,)),
+        ],
         compiler_params=pltpu.CompilerParams(vmem_limit_bytes=VMEM_LIMIT),
         name="finish",
     )(viscosity, outside, inside, outer, first, last, near)
@@ -288,11 +317,11 @@
     across += [(j, i) for i, j in across]
     within = [(i, i + 1) for i in range(0, size, 2)]
     within += [(j, i) for i, j in within]
-    outer = analyse(True, coarse, table, sources, members)
-    outside = lax.ppermute(outer, "lat", across)
-    inner = analyse(False, coarse, table, sources, members)
-    inside = lax.ppermute(inner, "lat", within)
-    first, last, near = begin(viscosity, inside, inner, outer)
+    outer, send = analyse(True, coarse, table, sources, members)
+    outside = lax.ppermute(send, "lat", across)
+    inner, send = analyse(False, coarse, table, sources, members)
+    inside = lax.ppermute(send, "lat", within)
+    first, last, near, inside = begin(viscosity, inside, inner, outer)
     out = finish(viscosity, outside, inside, outer, first, last, near)
     return out.reshape(members, fields, rows, lev, nlon)
 

time: 59.2 us -> 58.5 us (0.988)
  waiting for transfers between devices: 6.67 us -> 5.68 us
    ppermute x2, waiting for transfers between devices: 6.67 us -> 5.68 us  [the longest x1 4.2 us: on_device(): outside = lax.ppermute(send, 'lat', across)]
where the time goes in v6:
time: 58.5 us; the launch traced here: 58.3 us
  blocking collectives  41.5 us (71%)
  Pallas kernels  7.16 us (12%)
  waiting for transfers between devices  5.68 us (10%)
  starting transfers between devices  3.84 us (7%)
    all_gather x1, blocking collectives, on_device(): sources = lax.all_gather(picked, 'mem')  41.5 us
    ppermute x1, waiting for transfers between devices, on_device(): outside = lax.ppermute(send, 'lat', across)  4.2 us
    pallas_call x2, Pallas kernels, analyse(): pl.pallas_call(functools.partial(analysis_kernel, facing, 4), out_shape=(...  2.47 us
    pallas_call x1, Pallas kernels, finish(): pl.pallas_call(functools.partial(finish_kernel, GROUP), out_shape=jax.Sha...  1.95 us
    ppermute x1, starting transfers between devices, on_device(): inside = lax.ppermute(send, 'lat', within)  1.92 us
    ppermute x1, starting transfers between devices, on_device(): outside = lax.ppermute(send, 'lat', across)  1.92 us
    pallas_call x1, Pallas kernels, pick(): pl.pallas_call(pick_kernel, out_shape=(jax.ShapeDtypeStruct((src_ids.shap...  1.75 us
    ppermute x1, waiting for transfers between devices, on_device(): inside = lax.ppermute(send, 'lat', within)  1.48 us
  transfers between devices with their start and end apart: 2, of which 2 were waited for; matrix products, arithmetic and copies ran while one was open for 0% of the time, Pallas kernels for 4%

profile of v6, /device:TPU:64, one launch (start us, length us, event | category | flops | bytes accessed | tf_op | source)
XLA Modules:
  0.0 58.3 jit_solution(9204944753509388395)
XLA Ops:
  0.0 1.8 %pick.1 = (bf16[8,5,16,128]{3,2,1,0:T(8,128)(2,1)}, f32[2,96,256]{2,1,0:T(8,128)}) custom-call(s32[1,8]{1,0:T(1,128)} %ids_ref.1, bf16[16,5,16,128]{3,2,1,0:T(8,128)(2,1)} %bitcast.12, s32[1,128]{1,0:T(1,128)} %bitcast.13, f32[1,128]{1,0:T(1,128)} %bitcast.14), custom_call_target="tpu_custom_call" | custom-call | tf_op jit(solution)/shard_map/pick/pallas_call | solution.py:30
  1.8 0.0 copy-start.1
  1.8 0.0 copy-start.2
  1.8 41.5 %all-gather = bf16[32,5,16,128]{3,2,1,0:T(8,128)(2,1)S(1)} all-gather(bf16[8,5,16,128]{3,2,1,0:T(8,128)(2,1)} %get-tuple-element.16), channel_id=2, replica_groups=mesh['mem'=4,'lat'=256] {'mem'}, dimensions={0}, use_global_device_ids=true | all-gather | bytes 819200 | tf_op jit(solution)/shard_map/all_gather | solution.py:314
  43.3 0.0 copy-done.1
  43.3 0.0 copy-done.2
  43.3 1.2 %analysis_outer.1 = (f32[80,8,128]{2,1,0:T(8,128)S(1)}, bf16[61,16,128]{2,1,0:T(8,128)(2,1)S(1)}) custom-call(f32[512,32]{1,0:T(8,128)S(1)} %bitcast.10, f32[2,96,256]{2,1,0:T(8,128)S(1)} %copy-done.2, bf16[160,16,128]{2,1,0:T(8,128)(2,1)S(1)} %bitcast.8), custom_call_target="tpu_custom_call" | custom-call | flops 20000000000 | bytes 20000000 | tf_op jit(solution)/shard_map/analysis_outer/pallas_call | solution.py:139
  44.5 1.9 %collective-permute-start = (bf16[61,16,128]{2,1,0:T(8,128)(2,1)S(1)}, bf16[61,16,128]{2,1,0:T(8,128)(2,1)S(1)}, u32[]{:S(2)}, u32[]{:S(2)}) collective-permute-start(bf16[61,16,128]{2,1,0:T(8,128)(2,1)S(1)} %get-tuple-element.17), channel_id=1, source_target_pairs={{1,2},{3,4},{5,6},{7,8},{9,10},{11,12},{13,14},{15,16},{17,18},{19... | collective-permute-start | bytes 749576 | tf_op jit(solution)/shard_map/ppermute | solution.py:321
  46.5 1.2 %analysis_inner.1 = (f32[80,8,128]{2,1,0:T(8,128)S(1)}, bf16[60,16,128]{2,1,0:T(8,128)(2,1)S(1)}) custom-call(f32[512,32]{1,0:T(8,128)S(1)} %bitcast.11, f32[2,96,256]{2,1,0:T(8,128)S(1)} %copy-done.2, bf16[160,16,128]{2,1,0:T(8,128)(2,1)S(1)} %bitcast.9), custom_call_target="tpu_custom_call" | custom-call | flops 20000000000 | bytes 20000000 | tf_op jit(solution)/shard_map/analysis_inner/pallas_call | solution.py:139
  47.7 0.0 copy-start
  47.7 1.9 %collective-permute-start.1 = (bf16[60,16,128]{2,1,0:T(8,128)(2,1)S(1)}, bf16[60,16,128]{2,1,0:T(8,128)(2,1)S(1)}, u32[]{:S(2)}, u32[]{:S(2)}) collective-permute-start(bf16[60,16,128]{2,1,0:T(8,128)(2,1)S(1)} %get-tuple-element.18), channel_id=1, source_target_pairs={{0,1},{2,3},{4,5},{6,7},{8,9},{10,11},{12,13},{14,15},{16,17},{18,... | collective-permute-start | bytes 737288 | tf_op jit(solution)/shard_map/ppermute | solution.py:323
  49.6 1.5 %collective-permute-done.1.sent_ref = bf16[60,16,128]{2,1,0:T(8,128)(2,1)S(1)} collective-permute-done((bf16[60,16,128]{2,1,0:T(8,128)(2,1)S(1)}, bf16[60,16,128]{2,1,0:T(8,128)(2,1)S(1)}, u32[]{:S(2)}, u32[]{:S(2)}) %collective-permute-start.1) | collective-permute-done | bytes 245792 | tf_op jit(solution)/shard_map/ppermute | solution.py:323
  51.1 0.0 copy-done
  51.1 1.0 %begin.1 = (f32[80,8,128]{2,1,0:T(8,128)S(1)}, f32[80,8,128]{2,1,0:T(8,128)S(1)}, f32[80,8,128]{2,1,0:T(8,128)S(1)}, f32[80,8,128]{2,1,0:T(8,128)S(1)}) custom-call(f32[4,128]{1,0:T(4,128)S(1)} %copy-done, bf16[60,16,128]{2,1,0:T(8,128)(2,1)S(1)} %collective-permute-done.1.sent_ref, f32[80,8,128]{2,1,0:T(8,128)S(1)} %get-tuple-element.19.inner_ref, ...), custom_call_target="tpu_custom_call" | custom-call | flops 1 | bytes 1 | tf_op jit(solution)/shard_map/begin/pallas_call | solution.py:222
  52.1 4.2 %collective-permute-done.sent_ref = bf16[61,16,128]{2,1,0:T(8,128)(2,1)S(1)} collective-permute-done((bf16[61,16,128]{2,1,0:T(8,128)(2,1)S(1)}, bf16[61,16,128]{2,1,0:T(8,128)(2,1)S(1)}, u32[]{:S(2)}, u32[]{:S(2)}) %collective-permute-start) | collective-permute-done | bytes 249888 | tf_op jit(solution)/shard_map/ppermute | solution.py:321
  56.3 2.0 %finish.1 = f32[80,16,128]{2,1,0:T(8,128)} custom-call(f32[4,128]{1,0:T(4,128)S(1)} %copy-done, bf16[61,16,128]{2,1,0:T(8,128)(2,1)S(1)} %collective-permute-done.sent_ref, f32[80,8,128]{2,1,0:T(8,128)S(1)} %get-tuple-element.21.inside_ref, f32[80,8,128]{2,1,0:T(8,128)S(1)} %get-tuple-element.20.outer_ref, f32[80,8,128]{2,1,0:T(8,128)S(1)} %get-tuple-element.22.first_ref, ...), custom_call_target="tpu_custom_call" | custom-call | tf_op jit(solution)/shard_map/finish/pallas_call | solution.py:292
Async XLA Ops:
  1.8 41.5 %copy-start.1 = (f32[2,16,32,16]{2,3,1,0:T(8,128)S(1)}, f32[2,16,32,16]{2,3,1,0:T(8,128)}, u32[]{:S(2)}) copy-start(f32[2,16,32,16]{2,3,1,0:T(8,128)} %param.8) | copy-start | bytes 196612
  1.8 41.5 %copy-start.2 = (f32[2,96,256]{2,1,0:T(8,128)S(1)}, f32[2,96,256]{2,1,0:T(8,128)}, u32[]{:S(2)}) copy-start(f32[2,96,256]{2,1,0:T(8,128)} %get-tuple-element.15.refs_1_) | copy-start | bytes 589828
  44.5 11.8 %collective-permute-start = (bf16[61,16,128]{2,1,0:T(8,128)(2,1)S(1)}, bf16[61,16,128]{2,1,0:T(8,128)(2,1)S(1)}, u32[]{:S(2)}, u32[]{:S(2)}) collective-permute-start(bf16[61,16,128]{2,1,0:T(8,128)(2,1)S(1)} %get-tuple-element.17), channel_id=1, source_target_pairs={{1,2},{3,4},{5,6},{7,8},{9,10},{11,12},{13,14},{15,16},{17,18},{19... | collective-permute-start | bytes 749576 | tf_op jit(solution)/shard_map/ppermute | solution.py:321
  47.7 3.4 %copy-start = (f32[4,128]{1,0:T(4,128)S(1)}, f32[4,128]{1,0:T(4,128)}, u32[]{:S(2)}) copy-start(f32[4,128]{1,0:T(4,128)} %viscosity_ref.3) | copy-start | bytes 6148
  47.7 3.4 %collective-permute-start.1 = (bf16[60,16,128]{2,1,0:T(8,128)(2,1)S(1)}, bf16[60,16,128]{2,1,0:T(8,128)(2,1)S(1)}, u32[]{:S(2)}, u32[]{:S(2)}) collective-permute-start(bf16[60,16,128]{2,1,0:T(8,128)(2,1)S(1)} %get-tuple-element.18), channel_id=1, source_target_pairs={{0,1},{2,3},{4,5},{6,7},{8,9},{10,11},{12,13},{14,15},{16,17},{18,... | collective-permute-start | bytes 737288 | tf_op jit(solution)/shard_map/ppermute | solution.py:323

commit v7 on v6

--- a/solution.py
+++ b/solution.py
@@ -10,7 +10,7 @@
 ROWS = 4
 LEV = 4
 FIELDS = 5
-GROUP = 2
+GROUP = 4
 PAD = 1
 PARTS = 4
 VMEM_LIMIT = 48 * 1024 * 1024

time: 58.5 us -> 58.1 us (level)
  Pallas kernels: 7.16 us -> 6.48 us
  transfers between devices with their start and end apart: 2 -> 2, of which waited for: 2 -> 2; matrix products, arithmetic and copies ran while one was open for 0% -> 0% of each run, Pallas kernels for 4% -> 3%
where the time goes in v7:
time: 58.1 us; the launch traced here: 57.9 us
  blocking collectives  41.5 us (71%)
  Pallas kernels  6.48 us (11%)
  waiting for transfers between devices  5.97 us (10%)
  starting transfers between devices  3.84 us (7%)
    all_gather x1, blocking collectives, on_device(): sources = lax.all_gather(picked, 'mem')  41.5 us
    ppermute x1, waiting for transfers between devices, on_device(): outside = lax.ppermute(send, 'lat', across)  4.49 us
    pallas_call x2, Pallas kernels, analyse(): pl.pallas_call(functools.partial(analysis_kernel, facing, 4), out_shape=(...  2.47 us
    ppermute x1, starting transfers between devices, on_device(): outside = lax.ppermute(send, 'lat', across)  1.92 us
    ppermute x1, starting transfers between devices, on_device(): inside = lax.ppermute(send, 'lat', within)  1.92 us
    pallas_call x1, Pallas kernels, pick(): pl.pallas_call(pick_kernel, out_shape=(jax.ShapeDtypeStruct((src_ids.shap...  1.75 us
    pallas_call x1, Pallas kernels, finish(): pl.pallas_call(functools.partial(finish_kernel, GROUP), out_shape=jax.Sha...  1.57 us
    ppermute x1, waiting for transfers between devices, on_device(): inside = lax.ppermute(send, 'lat', within)  1.48 us
  transfers between devices with their start and end apart: 2, of which 2 were waited for; matrix products, arithmetic and copies ran while one was open for 0% of the time, Pallas kernels for 3%

profile of v7, /device:TPU:64, one launch (start us, length us, event | category | flops | bytes accessed | tf_op | source)
XLA Modules:
  0.0 57.9 jit_solution(9769120376975907592)
XLA Ops:
  0.0 1.8 %pick.1 = (bf16[8,5,16,128]{3,2,1,0:T(8,128)(2,1)}, f32[2,96,256]{2,1,0:T(8,128)}) custom-call(s32[1,8]{1,0:T(1,128)} %ids_ref.1, bf16[16,5,16,128]{3,2,1,0:T(8,128)(2,1)} %bitcast.12, s32[1,128]{1,0:T(1,128)} %bitcast.13, f32[1,128]{1,0:T(1,128)} %bitcast.14), custom_call_target="tpu_custom_call" | custom-call | tf_op jit(solution)/shard_map/pick/pallas_call | solution.py:30
  1.8 0.0 copy-start.1
  1.8 0.0 copy-start.2
  1.8 41.5 %all-gather = bf16[32,5,16,128]{3,2,1,0:T(8,128)(2,1)S(1)} all-gather(bf16[8,5,16,128]{3,2,1,0:T(8,128)(2,1)} %get-tuple-element.16), channel_id=2, replica_groups=mesh['mem'=4,'lat'=256] {'mem'}, dimensions={0}, use_global_device_ids=true | all-gather | bytes 819200 | tf_op jit(solution)/shard_map/all_gather | solution.py:314
  43.3 0.0 copy-done.1
  43.3 0.0 copy-done.2
  43.3 1.2 %analysis_outer.1 = (f32[80,8,128]{2,1,0:T(8,128)S(1)}, bf16[61,16,128]{2,1,0:T(8,128)(2,1)S(1)}) custom-call(f32[512,32]{1,0:T(8,128)S(1)} %bitcast.10, f32[2,96,256]{2,1,0:T(8,128)S(1)} %copy-done.2, bf16[160,16,128]{2,1,0:T(8,128)(2,1)S(1)} %bitcast.8), custom_call_target="tpu_custom_call" | custom-call | flops 20000000000 | bytes 20000000 | tf_op jit(solution)/shard_map/analysis_outer/pallas_call | solution.py:139
  44.5 1.9 %collective-permute-start = (bf16[61,16,128]{2,1,0:T(8,128)(2,1)S(1)}, bf16[61,16,128]{2,1,0:T(8,128)(2,1)S(1)}, u32[]{:S(2)}, u32[]{:S(2)}) collective-permute-start(bf16[61,16,128]{2,1,0:T(8,128)(2,1)S(1)} %get-tuple-element.17), channel_id=1, source_target_pairs={{1,2},{3,4},{5,6},{7,8},{9,10},{11,12},{13,14},{15,16},{17,18},{19... | collective-permute-start | bytes 749576 | tf_op jit(solution)/shard_map/ppermute | solution.py:321
  46.5 1.2 %analysis_inner.1 = (f32[80,8,128]{2,1,0:T(8,128)S(1)}, bf16[60,16,128]{2,1,0:T(8,128)(2,1)S(1)}) custom-call(f32[512,32]{1,0:T(8,128)S(1)} %bitcast.11, f32[2,96,256]{2,1,0:T(8,128)S(1)} %copy-done.2, bf16[160,16,128]{2,1,0:T(8,128)(2,1)S(1)} %bitcast.9), custom_call_target="tpu_custom_call" | custom-call | flops 20000000000 | bytes 20000000 | tf_op jit(solution)/shard_map/analysis_inner/pallas_call | solution.py:139
  47.7 0.0 copy-start
  47.7 1.9 %collective-permute-start.1 = (bf16[60,16,128]{2,1,0:T(8,128)(2,1)S(1)}, bf16[60,16,128]{2,1,0:T(8,128)(2,1)S(1)}, u32[]{:S(2)}, u32[]{:S(2)}) collective-permute-start(bf16[60,16,128]{2,1,0:T(8,128)(2,1)S(1)} %get-tuple-element.18), channel_id=1, source_target_pairs={{0,1},{2,3},{4,5},{6,7},{8,9},{10,11},{12,13},{14,15},{16,17},{18,... | collective-permute-start | bytes 737288 | tf_op jit(solution)/shard_map/ppermute | solution.py:323
  49.6 1.5 %collective-permute-done.1.sent_ref = bf16[60,16,128]{2,1,0:T(8,128)(2,1)S(1)} collective-permute-done((bf16[60,16,128]{2,1,0:T(8,128)(2,1)S(1)}, bf16[60,16,128]{2,1,0:T(8,128)(2,1)S(1)}, u32[]{:S(2)}, u32[]{:S(2)}) %collective-permute-start.1) | collective-permute-done | bytes 245792 | tf_op jit(solution)/shard_map/ppermute | solution.py:323
  51.1 0.0 copy-done
  51.1 0.7 %begin.1 = (f32[80,8,128]{2,1,0:T(8,128)S(1)}, f32[80,8,128]{2,1,0:T(8,128)S(1)}, f32[80,8,128]{2,1,0:T(8,128)S(1)}, f32[80,8,128]{2,1,0:T(8,128)S(1)}) custom-call(f32[4,128]{1,0:T(4,128)S(1)} %copy-done, bf16[60,16,128]{2,1,0:T(8,128)(2,1)S(1)} %collective-permute-done.1.sent_ref, f32[80,8,128]{2,1,0:T(8,128)S(1)} %get-tuple-element.19.inner_ref, ...), custom_call_target="tpu_custom_call" | custom-call | flops 1 | bytes 1 | tf_op jit(solution)/shard_map/begin/pallas_call | solution.py:222
  51.8 4.5 %collective-permute-done.sent_ref = bf16[61,16,128]{2,1,0:T(8,128)(2,1)S(1)} collective-permute-done((bf16[61,16,128]{2,1,0:T(8,128)(2,1)S(1)}, bf16[61,16,128]{2,1,0:T(8,128)(2,1)S(1)}, u32[]{:S(2)}, u32[]{:S(2)}) %collective-permute-start) | collective-permute-done | bytes 249888 | tf_op jit(solution)/shard_map/ppermute | solution.py:321
  56.3 1.6 %finish.1 = f32[80,16,128]{2,1,0:T(8,128)} custom-call(f32[4,128]{1,0:T(4,128)S(1)} %copy-done, bf16[61,16,128]{2,1,0:T(8,128)(2,1)S(1)} %collective-permute-done.sent_ref, f32[80,8,128]{2,1,0:T(8,128)S(1)} %get-tuple-element.21.inside_ref, f32[80,8,128]{2,1,0:T(8,128)S(1)} %get-tuple-element.20.outer_ref, f32[80,8,128]{2,1,0:T(8,128)S(1)} %get-tuple-element.22.first_ref, ...), custom_call_target="tpu_custom_call" | custom-call | tf_op jit(solution)/shard_map/finish/pallas_call | solution.py:292
Async XLA Ops:
  1.8 41.5 %copy-start.1 = (f32[2,16,32,16]{2,3,1,0:T(8,128)S(1)}, f32[2,16,32,16]{2,3,1,0:T(8,128)}, u32[]{:S(2)}) copy-start(f32[2,16,32,16]{2,3,1,0:T(8,128)} %param.8) | copy-start | bytes 196612
  1.8 41.5 %copy-start.2 = (f32[2,96,256]{2,1,0:T(8,128)S(1)}, f32[2,96,256]{2,1,0:T(8,128)}, u32[]{:S(2)}) copy-start(f32[2,96,256]{2,1,0:T(8,128)} %get-tuple-element.15.refs_1_) | copy-start | bytes 589828
  44.5 11.8 %collective-permute-start = (bf16[61,16,128]{2,1,0:T(8,128)(2,1)S(1)}, bf16[61,16,128]{2,1,0:T(8,128)(2,1)S(1)}, u32[]{:S(2)}, u32[]{:S(2)}) collective-permute-start(bf16[61,16,128]{2,1,0:T(8,128)(2,1)S(1)} %get-tuple-element.17), channel_id=1, source_target_pairs={{1,2},{3,4},{5,6},{7,8},{9,10},{11,12},{13,14},{15,16},{17,18},{19... | collective-permute-start | bytes 749576 | tf_op jit(solution)/shard_map/ppermute | solution.py:321
  47.7 3.4 %copy-start = (f32[4,128]{1,0:T(4,128)S(1)}, f32[4,128]{1,0:T(4,128)}, u32[]{:S(2)}) copy-start(f32[4,128]{1,0:T(4,128)} %viscosity_ref.3) | copy-start | bytes 6148
  47.7 3.4 %collective-permute-start.1 = (bf16[60,16,128]{2,1,0:T(8,128)(2,1)S(1)}, bf16[60,16,128]{2,1,0:T(8,128)(2,1)S(1)}, u32[]{:S(2)}, u32[]{:S(2)}) collective-permute-start(bf16[60,16,128]{2,1,0:T(8,128)(2,1)S(1)} %get-tuple-element.18), channel_id=1, source_target_pairs={{0,1},{2,3},{4,5},{6,7},{8,9},{10,11},{12,13},{14,15},{16,17},{18,... | collective-permute-start | bytes 737288 | tf_op jit(solution)/shard_map/ppermute | solution.py:323
